TPU v7x, 256 devices: a whole 4x4x8 slice. The times are simulated.
256 devices in a mesh: tm: 2 (over z_lo), lat: 16 (over z_hi, y), lon: 8 (over x, core).
Axes of the slice: x: 4, y: 4, z: 8 (z_hi: 4, z_lo: 2; z = z_hi * 2 + z_lo), core: 2. Of those that a mesh axis runs over, the one named last changes fastest.
Arguments:
- control: bfloat16 [1024, 2, 4, 8, 2048], P('lat', 'tm', None, None, 'lon'), may hold values from -6 to 6
- deviations: float32 [1024, 2, 4, 8, 2048], P('lat', 'tm', None, None, 'lon'), may hold values from 0.3 to 3
- increments: float32 [1024, 2, 4, 8, 2048], P('lat', 'tm', None, None, 'lon'), may hold values from -6 to 6
- lon_corr: bfloat16 [2048, 2048], P('lon'), may hold values from -0.125 to 0.125
- lat_corr: bfloat16 [1024, 1024], P('lat'), may hold values from -0.1875 to 0.1875
- offsets: int32 [2, 8], replicated, may hold values from -2 to 2, as said below
- courant: float32 [4], replicated, may hold values from 0.2 to 0.8
Outputs:
- misfit: float32 [1024, 2, 4, 8, 2048], P('lat', 'tm', None, None, 'lon')
Inputs may be any that keep to these rules, and one draw needn't show every extreme that they name: `offsets`: each of the two rows holds both -2 and 2.
All inputs are finite; a program needn't handle non-finite values.
Results may differ from a plain program's by a relative error of at most 0.0024.
Values may be sent and summed in bfloat16 or wider, within the bound.
No kernel may reach another device: no remote copies, remote signals or barrier semaphores. Data moves between devices by JAX's collectives and lax.ppermute only.
A program may use at most 128 MiB of HBM per device.

v0:
```python
import jax
import jax.numpy as jnp
from jax import lax
from jax.sharding import PartitionSpec as P


def with_halo(block, sides, width, periodic):
    for axis, dim in sides:
        count = lax.axis_size(axis)
        forward = [(i, i + 1) for i in range(count - 1)]
        if periodic:
            forward.append((count - 1, 0))
        backward = [(target, source) for source, target in forward]
        low = lax.ppermute(
            lax.slice_in_dim(block, block.shape[dim] - width, None, axis=dim), axis, forward
        )
        high = lax.ppermute(lax.slice_in_dim(block, 0, width, axis=dim), axis, backward)
        block = jnp.concatenate([low, block, high], axis=dim)
    return block


def from_behind(value, axis, steps):
    count = lax.axis_size(axis)
    initial, last = (max(0, -steps), min(count, count - steps))
    return lax.ppermute(value, axis, [(source, source + steps) for source in range(initial, last)])


def advect(field_now, offsets, courant):
    widened = with_halo(field_now.astype(jnp.bfloat16), (("lon", 4),), 2, True).astype(
        field_now.dtype
    )
    padded = with_halo(widened.astype(jnp.bfloat16), (("lat", 0),), 2, False).astype(widened.dtype)
    lat_count = field_now.shape[0]
    lon_count = field_now.shape[4]
    displaced_all = []
    for level_idx in range(field_now.shape[3]):
        one_level = padded[:, :, :, level_idx, :]
        displaced = lax.dynamic_slice_in_dim(one_level, 2 - offsets[0, level_idx], lat_count, 0)
        displaced = lax.dynamic_slice_in_dim(displaced, 2 - offsets[1, level_idx], lon_count, 3)
        displaced_all.append(displaced)
    shifted = jnp.stack(displaced_all, axis=3)
    blending = courant.reshape(1, 1, -1, 1, 1)
    return (1.0 - blending) * field_now + blending * shifted


def body(control, deviations, increments, lon_corr, lat_corr, offsets, courant):
    lat_count = control.shape[0]
    lon_count = control.shape[4]
    flat_rows = control.reshape(-1, lon_count)
    smoothed = lax.dot_general(
        lax.all_gather(flat_rows, "lon", axis=1, tiled=True),
        lon_corr,
        (((1,), (1,)), ((), ())),
        preferred_element_type=jnp.float32,
    )
    halfway = smoothed.astype(jnp.bfloat16).reshape(lat_count, -1)
    correlated = jnp.dot(
        lat_corr,
        lax.all_gather(halfway, "lat", axis=0, tiled=True),
        preferred_element_type=jnp.float32,
    )
    forcing = deviations * correlated.reshape(control.shape)
    evolved = advect(increments, offsets, courant)
    carried = from_behind(evolved, "tm", 1)
    previous = jnp.concatenate([carried, evolved[:, :-1]], axis=1)
    return increments - previous - forcing


def solution(mesh):
    in_specs = (
        P("lat", "tm", None, None, "lon"),
        P("lat", "tm", None, None, "lon"),
        P("lat", "tm", None, None, "lon"),
        P("lon", None),
        P("lat", None),
        P(),
        P(),
    )
    out_specs = P("lat", "tm", None, None, "lon")
    return jax.shard_map(body, mesh=mesh, in_specs=in_specs, out_specs=out_specs, check_vma=False)
```

profile of v0, /device:TPU:1, one launch (start us, length us, event | category | flops | bytes accessed | tf_op | source)
XLA Modules:
  0.0 348.5 jit_solution(18185432202559513910)
XLA Ops:
  6.5 0.0 copy-start
  6.5 0.0 all-gather.3.cloned.1.call-start
  6.5 0.7 all-gather.3.cloned.1.call-update
  7.3 0.0 all-gather.5.cloned.1.call-start
  7.3 62.6 %all-gather.3.cloned.1.call-done = bf16[2048,2048]{1,0:T(8,128)(2,1)} async-done(((bf16[2048,256]{1,0:T(8,128)(2,1)}), bf16[2048,2048]{1,0:T(8,128)(2,1)}) %all-gather.3.cloned.1.call-update) | async-done | bytes 8388624 | tf_op jit(solution)/shard_map/all_gather | solution.py:51
  69.9 0.0 copy-done
  69.9 6.7 %convolution_convert_fusion = bf16[2048,256]{1,0:T(8,128)(2,1)} fusion(bf16[2048,2048]{1,0:T(8,128)(2,1)} %all-gather.3.cloned.1.call-done, bf16[256,2048]{1,0:T(8,128)(2,1)S(1)} %copy-done), kind=kOutput, calls=%fused_computation | convolution fusion | flops 2148007936 | bytes 10485760 | tf_op jit(solution)/shard_map/dot_general | solution.py:50
  76.6 0.0 copy-start.1
  76.6 2.5 reshape.246
  79.1 0.0 all-gather.5.cloned.1.call-update
  79.1 0.0 copy-done.1
  79.2 0.0 copy-start.8
  79.2 0.2 convert_element_type.19
  79.3 0.0 copy-start.2
  79.3 0.0 copy-start.7
  79.4 0.3 fusion.2
  79.6 1.3 collective-permute-start
  81.0 0.0 collective-permute-start.1
  81.0 0.0 copy-done.8
  81.0 6.1 %collective-permute-done = bf16[64,1,4,8,2]{4,3,2,1,0:T(8,128)(2,1)S(1)} collective-permute-done((bf16[64,1,4,8,2]{4,3,2,1,0:T(8,128)(2,1)S(1)}, bf16[64,1,4,8,2]{4,3,2,1,0:T(8,128)(2,1)S(1)}, u32[]{:S(2)}, u32[]{:S(2)}) %collective-permute-start) | collective-permute-done | bytes 8224 | tf_op jit(solution)/shard_map/ppermute | solution.py:14
  87.1 0.0 copy-start.4
  87.1 2.5 collective-permute-done.1
  89.6 0.0 copy-start.5
  89.6 0.1 pad_maximum_fusion.2
  89.7 0.0 copy-done.2
  89.7 0.0 copy-done.4
  89.7 3.1 collective-permute-start.2
  92.8 0.0 copy-done.5
  92.8 1.3 collective-permute-start.3
  94.1 0.0 copy-done.7
  94.1 0.7 fusion.3
  115.3 0.0 collective-permute-done.2
  115.3 0.0 collective-permute-done.3
  115.3 2.4 maximum_convert_fusion
  117.7 2.3 fusion.1
  119.9 1.8 constant_dynamic-slice_fusion
  121.8 2.0 constant_dynamic-slice_fusion.2
  123.7 2.0 constant_dynamic-slice_fusion.4
  125.7 2.0 constant_dynamic-slice_fusion.6
  127.7 6.5 %stack.2 = f32[64,1,4,8,256]{4,3,2,1,0:T(8,128)} concatenate(f32[64,1,4,1,256]{4,3,2,1,0:T(1,128)} %get-tuple-element.40, f32[64,1,4,1,256]{4,3,2,1,0:T(1,128)} %get-tuple-element.39, f32[64,1,4,1,256]{4,3,2,1,0:T(1,128)} %get-tuple-element.38, f32[64,1,4,1,256]{4,3,2,1,0:T(1,128)} %get-tuple-element.37, f32[64,1,4,1,256]{4,3,2,1,0:T(1,128)} %get-tuple-element.36, ...), dimensions={3} | concatenate | bytes 4194304 | tf_op jit(solution)/shard_map/stack | solution.py:41
  134.2 0.0 copy-start.6
  134.2 3.7 %multiply_add_fusion = f32[64,1,4,8,256]{4,3,2,1,0:T(8,128)} fusion(f32[64,1,4,8,256]{4,3,2,1,0:T(8,128)} %stack.2, f32[64,1,4,8,256]{4,3,2,1,0:T(8,128)S(1)} %copy-done.1, f32[4]{0:T(128)S(1)} %copy-done.8, f32[4]{0:T(128)S(1)} %broadcast_subtract_fusion), kind=kLoop, calls=%fused_computation.3 | loop fusion | flops 1572864 | bytes 6291488 | tf_op jit(solution)/shard_map/add | solution.py:43
  137.8 4.5 %collective-permute-start.4 = (f32[64,1,4,8,256]{4,3,2,1,0:T(8,128)}, f32[64,1,4,8,256]{4,3,2,1,0:T(8,128)}, u32[]{:S(2)}, u32[]{:S(2)}) collective-permute-start(f32[64,1,4,8,256]{4,3,2,1,0:T(8,128)} %multiply_add_fusion), channel_id=1, source_target_pairs={{0,128},{1,129},{2,130},{3,131},{4,132},{5,133},{6,134},{7,135},{8... | collective-permute-start | bytes 6291464 | tf_op jit(solution)/shard_map/ppermute | solution.py:25
  142.4 185.0 %all-gather.5.cloned.1.call-done = bf16[1024,8192]{1,0:T(8,128)(2,1)} async-done(((bf16[64,8192]{1,0:T(8,128)(2,1)}), bf16[1024,8192]{1,0:T(8,128)(2,1)}) %all-gather.5.cloned.1.call-update) | async-done | bytes 16777232 | tf_op jit(solution)/shard_map/all_gather | solution.py:59
  327.4 0.0 copy-done.6
  327.4 8.8 %fusion.4 = f32[8192,64]{0,1:T(8,128)S(1)} fusion(bf16[64,1024]{1,0:T(8,128)(2,1)S(1)} %copy-done.6, bf16[1024,8192]{1,0:T(8,128)(2,1)} %all-gather.5.cloned.1.call-done), kind=kOutput, calls=%fused_computation.20 | convolution fusion | flops 1073741824 | bytes 19005440 | tf_op jit(solution)/shard_map/dot_general | solution.py:57
  336.2 0.0 copy-start.3
  336.2 0.6 copy.9
  336.8 0.0 collective-permute-done.4
  336.8 0.9 copy-done.3
  337.8 3.9 %fusion = f32[64,1,4,8,256]{4,3,2,1,0:T(8,128)} fusion(f32[64,1,4,8,256]{4,3,2,1,0:T(8,128)S(1)} %copy-done.3, f32[64,1,4,8,256]{4,3,2,0,1:T(8,128)S(1)} %bitcast.46, f32[64,1,4,8,256]{4,3,2,1,0:T(8,128)S(1)} %copy-done.1, f32[64,1,4,8,256]{4,3,2,1,0:T(8,128)} %collective-permute-done.4), kind=kLoop, calls=%fused_computation.2 | loop fusion | flops 1572864 | bytes 10485760 | tf_op jit(solution)/shard_map/sub | solution.py:66
  (1 shorter events, 0.0 us)
Async XLA Ops:
  6.5 63.4 %copy-start = (bf16[256,2048]{1,0:T(8,128)(2,1)S(1)}, bf16[256,2048]{1,0:T(8,128)(2,1)}, u32[]{:S(2)}) copy-start(bf16[256,2048]{1,0:T(8,128)(2,1)} %param.10) | copy-start | bytes 3145732
  6.5 63.4 %all-gather.3.cloned.1.call-start = ((), (), s32[]{:S(2)}) async-start(), calls=%async_computation | async-start | bytes 9437184 | tf_op jit(solution)/shard_map/all_gather | solution.py:51
  7.3 320.1 %all-gather.5.cloned.1.call-start = ((), (), s32[]{:S(2)}) async-start(), calls=%async_computation.1 | async-start | bytes 17825792 | tf_op jit(solution)/shard_map/all_gather | solution.py:59
  76.6 2.5 copy-start.1
  79.2 1.8 copy-start.8
  79.3 10.3 %copy-start.2 = (bf16[64,1,4,8,256]{4,3,2,1,0:T(8,128)(2,1)}, bf16[64,1,4,8,256]{4,3,2,1,0:T(8,128)(2,1)S(1)}, u32[]{:S(2)}) copy-start(bf16[64,1,4,8,256]{4,3,2,1,0:T(8,128)(2,1)S(1)} %convert_element_type.19) | copy-start | bytes 3145732
  79.3 14.8 %copy-start.7 = (s32[2,8]{1,0:T(2,128)S(1)}, s32[2,8]{1,0:T(2,128)}, u32[]{:S(2)}) copy-start(s32[2,8]{1,0:T(2,128)} %param.12) | copy-start | bytes 196
  79.6 7.5 %collective-permute-start = (bf16[64,1,4,8,2]{4,3,2,1,0:T(8,128)(2,1)S(1)}, bf16[64,1,4,8,2]{4,3,2,1,0:T(8,128)(2,1)S(1)}, u32[]{:S(2)}, u32[]{:S(2)}) collective-permute-start(bf16[64,1,4,8,2]{4,3,2,1,0:T(8,128)(2,1)S(1)} %get-tuple-element.15), channel_id=1, source_target_pairs={{0,1},{1,2},{2,3},{3,4},{4,5},{5,6},{6,7},{7,0},{8,9},{9,10},{10,1... | collective-permute-start | bytes 24584 | tf_op jit(solution)/shard_map/ppermute | solution.py:14
  81.0 8.6 %collective-permute-start.1 = (bf16[64,1,4,8,2]{4,3,2,1,0:T(8,128)(2,1)S(1)}, bf16[64,1,4,8,2]{4,3,2,1,0:T(8,128)(2,1)S(1)}, u32[]{:S(2)}, u32[]{:S(2)}) collective-permute-start(bf16[64,1,4,8,2]{4,3,2,1,0:T(8,128)(2,1)S(1)} %get-tuple-element.16), channel_id=1, source_target_pairs={{1,0},{2,1},{3,2},{4,3},{5,4},{6,5},{7,6},{0,7},{9,8},{10,9},{11,1... | collective-permute-start | bytes 24584 | tf_op jit(solution)/shard_map/ppermute | solution.py:17
  87.1 2.6 copy-start.4
  89.6 3.3 copy-start.5
  89.7 25.6 %collective-permute-start.2 = (bf16[2,1,4,8,260]{4,3,2,1,0:T(8,128)(2,1)S(1)}, bf16[2,1,4,8,260]{4,3,2,1,0:T(8,128)(2,1)S(1)}, u32[]{:S(2)}, u32[]{:S(2)}) collective-permute-start(bf16[2,1,4,8,260]{4,3,2,1,0:T(8,128)(2,1)S(1)} %get-tuple-element.13), channel_id=1, source_target_pairs={{0,8},{8,16},{16,24},{24,32},{32,40},{40,48},{48,56},{56,64},{64,7... | collective-permute-start | bytes 99848 | tf_op jit(solution)/shard_map/ppermute | solution.py:14
  92.8 22.4 %collective-permute-start.3 = (bf16[2,1,4,8,260]{4,3,2,1,0:T(8,128)(2,1)S(1)}, bf16[2,1,4,8,260]{4,3,2,1,0:T(8,128)(2,1)S(1)}, u32[]{:S(2)}, u32[]{:S(2)}) collective-permute-start(bf16[2,1,4,8,260]{4,3,2,1,0:T(8,128)(2,1)S(1)} %get-tuple-element.14), channel_id=1, source_target_pairs={{8,0},{16,8},{24,16},{32,24},{40,32},{48,40},{56,48},{64,56},{72,6... | collective-permute-start | bytes 99848 | tf_op jit(solution)/shard_map/ppermute | solution.py:17
  134.2 193.2 %copy-start.6 = (bf16[64,1024]{1,0:T(8,128)(2,1)S(1)}, bf16[64,1024]{1,0:T(8,128)(2,1)}, u32[]{:S(2)}) copy-start(bf16[64,1024]{1,0:T(8,128)(2,1)} %param.11) | copy-start | bytes 393220
  137.8 199.0 %collective-permute-start.4 = (f32[64,1,4,8,256]{4,3,2,1,0:T(8,128)}, f32[64,1,4,8,256]{4,3,2,1,0:T(8,128)}, u32[]{:S(2)}, u32[]{:S(2)}) collective-permute-start(f32[64,1,4,8,256]{4,3,2,1,0:T(8,128)} %multiply_add_fusion), channel_id=1, source_target_pairs={{0,128},{1,129},{2,130},{3,131},{4,132},{5,133},{6,134},{7,135},{8... | collective-permute-start | bytes 6291464 | tf_op jit(solution)/shard_map/ppermute | solution.py:25
  336.2 1.6 copy-start.3
Sparse Core Ops, SparseCore 0:
  9.2 60.6 all-gather.2
  79.3 248.0 all-gather.4
where the time goes:
time: 350 us; the launch traced here: 348 us
  waiting for transfers between devices  257 us (73%)
  between operations  34 us (10%)
  local copies, waits for them, and re-layouts  21.6 us (6%)
  matrix products  15.5 us (4%)
  starting transfers between devices  10.3 us (3%)
  other arithmetic  10.2 us (3%)
    all_gather x1, waiting for transfers between devices, body(): lax.all_gather(halfway, 'lat', axis=0, tiled=True)  185 us
    all_gather x1, waiting for transfers between devices, body(): lax.all_gather(flat_rows, 'lon', axis=1, tiled=True)  62.6 us
    dot_general x1, matrix products, body(): jnp.dot(lat_corr, lax.all_gather(halfway, 'lat', axis=0, tiled=True), pre...  8.78 us
    dynamic_slice x4, local copies, waits for them, and re-layouts, advect(): lax.dynamic_slice_in_dim(displaced, 2 - offsets[1, level_idx], lon_count, 3)  7.71 us
  transfers between devices with their start and end apart: 7, of which 4 were waited for; matrix products, arithmetic and copies ran while one was open for 10% of the time, Pallas kernels for 0%

commit v1 on v0

v1 whole, which is shorter than its diff:
```python
import functools

import jax
import jax.numpy as jnp
from jax import lax
from jax.experimental import pallas as pl
from jax.experimental.pallas import tpu as pltpu
from jax.sharding import Mesh, PartitionSpec as P

F32, BF16 = jnp.float32, jnp.bfloat16
VMEM_LIMIT = 48 * 1024 * 1024
NT = (((1,), (1,)), ((), ()))


def call(kernel, out_shape, n_in, smem=(), scratch=(), before=(), work=0):
    def run(*refs):
        kernel(*refs[:n_in], *refs[n_in + len(before) :])

    in_specs = [
        pl.BlockSpec(memory_space=pltpu.SMEM if k in smem else pltpu.VMEM) for k in range(n_in)
    ] + [pl.BlockSpec(memory_space=pl.ANY)] * len(before)
    made = pl.pallas_call(
        run,
        out_shape=out_shape,
        in_specs=in_specs,
        out_specs=jax.tree.map(lambda _: pl.BlockSpec(memory_space=pltpu.VMEM), out_shape),
        scratch_shapes=list(scratch),
        compiler_params=pltpu.CompilerParams(vmem_limit_bytes=VMEM_LIMIT),
        cost_estimate=pl.CostEstimate(flops=0, bytes_accessed=work, transcendentals=0),
    )
    return lambda *args: made(*args, *before)


def after(value, *before):
    anywhere = pl.BlockSpec(memory_space=pl.ANY)
    return pl.pallas_call(
        lambda *refs: None,
        out_shape=jax.ShapeDtypeStruct(value.shape, value.dtype),
        in_specs=[anywhere] * (1 + len(before)),
        out_specs=anywhere,
        input_output_aliases={0: 0},
    )(value, *before)


def split_kernel(control, out, wide):
    for side in range(2):
        at = slice(side * 128, (side + 1) * 128)
        wide[side] = control[:, 0, :, at].astype(F32).reshape(512, 128)
    for level in range(8):
        for side in range(2):
            at = slice(side * 128, (side + 1) * 128)
            rows = wide[side, pl.ds(level, 64, stride=8), :].astype(BF16)
            out[level * 4 : (level + 1) * 4, :, at] = rows.reshape(4, 16, 128)


def smooth_kernel(place, mine, other, own, behind, ahead, across, keep, send):
    core, side = place[4], place[5]
    for k in range(4):
        corr = (own, behind, ahead, across)[k]
        for rows, at in ((mine, core), (other, 1 - core)):
            total = None
            for q in range(8):
                term = lax.dot_general(
                    rows[:, q].reshape(256, 256),
                    corr[:, q * 256 : (q + 1) * 256],
                    NT,
                    preferred_element_type=F32,
                )
                total = term if total is None else total + term
            total = total.astype(BF16)
            low, high = total[:, :128], total[:, 128:]
            keep[place[k], at] = jnp.where(side == 0, low, high)
            send[place[k], at] = jnp.where(side == 0, high, low)


def correlate_kernel(place, lat, kept, got, out):
    side = place[5]
    for block in range(4):
        at = slice(block * 256, (block + 1) * 256)
        for pair in range(2):
            total = None
            for cols, where in ((kept, side), (got, 1 - side)):
                for part in range(2):
                    left = lat[at, pl.ds(pl.multiple_of((where * 2 + part) * 256, 256), 256)]
                    right = jnp.concatenate([cols[pair * 2, part], cols[pair * 2 + 1, part]], axis=1)
                    term = jnp.dot(left, right, preferred_element_type=F32)
                    total = term if total is None else total + term
            total = total.astype(BF16)
            for k in range(4):
                for j in range(2):
                    out[(block * 4 + k) * 4 + pair * 2 + j] = total[
                        k * 64 : (k + 1) * 64, j * 128 : (j + 1) * 128
                    ]


def advect_kernel(inc, field, low, high, left, right, off0, off1, courant, out, padded):
    lane = lax.broadcasted_iota(jnp.int32, (4, 8, 128), 2)

    def fill(a, _):
        padded[a + 2, :, :, :256] = field[a].astype(F32)
        return 0

    lax.fori_loop(0, 64, fill, 0)
    padded[0:2, :, :, :256] = low[...].astype(F32)
    padded[66:68, :, :, :256] = high[...].astype(F32)

    def rim(a, _):
        padded[a, :, :, 256:] = jnp.where(lane < 64, right[a].astype(F32), left[a].astype(F32))
        return 0

    lax.fori_loop(0, 68, rim, 0)
    row_off = jnp.broadcast_to(off0[...][None], (4, 8, 384))
    col_off = jnp.broadcast_to(off1[...][None], (4, 8, 384))
    blend = courant[...]

    def step(a, _):
        at = padded[a + 2]
        moved = at
        for d in (-2, -1, 1, 2):
            moved = jnp.where(row_off == d, padded[a + 2 - d], moved)
        shifted = moved
        for d in (-2, -1, 1, 2):
            rolled = pltpu.roll(moved.reshape(32, 384), d % 384, 1).reshape(4, 8, 384)
            shifted = jnp.where(col_off == d, rolled, shifted)
        evolved = (1.0 - blend) * at[:, :, :256] + blend * shifted[:, :, :256]
        out[a] = inc[a] - evolved
        return 0

    lax.fori_loop(0, 64, step, 0)


def final_kernel(base, dev, got, out, acc):
    rows = base.shape[0]
    for v in range(4):
        for half in range(2):
            at = slice(half * 128, (half + 1) * 128)
            for level in range(8):
                row = got[(v * 8 + level) * 2 + half].astype(F32)
                acc[half, pl.ds(level, rows, stride=8), :] = row
            corr = acc[half].reshape(rows, 8, 128)
            out[:, v, :, at] = base[:, v, :, at] - dev[:, v, :, at] * corr


def body(control, deviations, increments, lon_corr, lat_corr, offsets, courant):
    x, c = lax.axis_index("x"), lax.axis_index("c")
    swap = [(0, 1), (1, 0)]
    lats = ("zh", "y")

    def along_x(v, s):
        return lax.ppermute(v, "x", [(i, (i + s) % 4) for i in range(4)])

    behind, ahead, across = (along_x(lon_corr, s) for s in (1, -1, 2))
    place = jnp.stack([x, (x + 3) % 4, (x + 1) % 4, (x + 2) % 4, c, x % 2]).astype(jnp.int32)

    parts = pl.pallas_call(
        split_kernel,
        grid=(4,),
        out_shape=jax.ShapeDtypeStruct((128, 16, 256), BF16),
        in_specs=[pl.BlockSpec((64, 1, 8, 256), lambda v: (0, v, 0, 0))],
        out_specs=pl.BlockSpec((32, 16, 256), lambda v: (v, 0, 0)),
        scratch_shapes=[pltpu.VMEM((2, 512, 128), F32)],
        compiler_params=pltpu.CompilerParams(vmem_limit_bytes=VMEM_LIMIT),
        cost_estimate=pl.CostEstimate(flops=0, bytes_accessed=0, transcendentals=0),
    )(control.reshape(64, 4, 8, 256))
    mine = lax.all_to_all(parts, ("zh", "y", "x", "c"), 0, 0, tiled=True)
    mine = mine.reshape(16, 8, 16, 256)
    other = lax.ppermute(mine, "c", swap)

    lat = lat_corr.reshape(64, 16, 4, 16).transpose(0, 2, 1, 3).reshape(64, 1024)
    lat = lax.all_gather(lat, lats, axis=0, tiled=True)

    inc = increments.reshape(64, 4, 8, 256)
    dev = deviations.reshape(64, 4, 8, 256)
    field = lax.ppermute(after(inc.astype(BF16), mine), "tm", [(0, 1)])
    low = lax.ppermute(field[62:], lats, [(i, i + 1) for i in range(15)])
    high = lax.ppermute(field[:2], lats, [(i + 1, i) for i in range(15)])
    wide = jnp.concatenate([low, field, high], axis=0)
    ring = [(i, (i + 1) % 8) for i in range(8)]
    back = [((i + 1) % 8, i) for i in range(8)]
    left = lax.ppermute(wide[..., 128:], ("x", "c"), ring)
    right = lax.ppermute(wide[..., :128], ("x", "c"), back)
    off = jnp.broadcast_to(offsets[:, :, None], (2, 8, 384))
    base = call(
        advect_kernel,
        jax.ShapeDtypeStruct((64, 4, 8, 256), F32),
        9,
        scratch=[pltpu.VMEM((68, 4, 8, 384), F32)],
        work=30_000_000,
    )(
        inc, field, low, high, left, right, off[0], off[1],
        jnp.broadcast_to(courant[:, None, None], (4, 8, 256)),
    )

    half = jax.ShapeDtypeStruct((4, 2, 256, 128), BF16)
    keep, send = call(smooth_kernel, (half, half), 7, smem=(0,))(
        place, mine, other, lon_corr, behind, ahead, across
    )
    got = lax.ppermute(send, "x", [(i, i ^ 1) for i in range(4)])
    res = call(
        correlate_kernel, jax.ShapeDtypeStruct((64, 64, 128), BF16), 4, smem=(0,), before=(field,)
    )(place, lat, keep, got)
    res = lax.all_to_all(res, ("zh", "y", "x"), 0, 0, tiled=True)

    big = pl.BlockSpec((16, 4, 8, 256), lambda i: (i, 0, 0, 0))
    out = pl.pallas_call(
        final_kernel,
        grid=(4,),
        out_shape=jax.ShapeDtypeStruct((64, 4, 8, 256), F32),
        in_specs=[big, big, pl.BlockSpec((64, 16, 128), lambda i: (0, i, 0))],
        out_specs=big,
        scratch_shapes=[pltpu.VMEM((2, 128, 128), F32)],
        compiler_params=pltpu.CompilerParams(vmem_limit_bytes=VMEM_LIMIT),
        cost_estimate=pl.CostEstimate(flops=0, bytes_accessed=0, transcendentals=0),
    )(base, dev, res)
    return out.reshape(increments.shape)


def solution(mesh):
    fine = Mesh(mesh.devices.reshape(2, 4, 4, 4, 2), ("tm", "zh", "y", "x", "c"))
    lat, lon = ("zh", "y"), ("x", "c")
    tile = P(lat, "tm", None, None, lon)
    in_specs = (tile, tile, tile, P(lon, None), P(lat, None), P(), P())
    return jax.shard_map(body, mesh=fine, in_specs=in_specs, out_specs=tile, check_vma=False)
```

time: 350 us -> 181 us (0.52)
  the two profiles are of different devices: /device:TPU:1 before, /device:TPU:95 now
where the time goes in v1:
time: 181 us
  waiting for transfers between devices  91.6 us (51%)
  starting transfers between devices  42 us (23%)
  Pallas kernels  23.9 us (13%)
  between operations  13.6 us (8%)
  local copies, waits for them, and re-layouts  6.96 us (4%)
  other arithmetic  2.8 us (2%)
    all_to_all x1, waiting for transfers between devices, body(): mine = lax.all_to_all(parts, ('zh', 'y', 'x', 'c'), 0, 0, tiled=True)  29 us
    ppermute x3, waiting for transfers between devices, along_x(): return lax.ppermute(v, 'x', [(i, (i + s) % 4) for i in range(4)])  20.7 us
    pallas_call x3, Pallas kernels, call(): return lambda *args: made(*args, *before)  18 us
    all_to_all x1, starting transfers between devices, body(): mine = lax.all_to_all(parts, ('zh', 'y', 'x', 'c'), 0, 0, tiled=True)  14.9 us
    ppermute x1, waiting for transfers between devices, body(): low = lax.ppermute(field[62:], lats, [(i, i + 1) for i in range(15)])  14.7 us
    all_to_all x1, starting transfers between devices, body(): res = lax.all_to_all(res, ('zh', 'y', 'x'), 0, 0, tiled=True)  12.6 us
    ppermute x1, waiting for transfers between devices, body(): field = lax.ppermute(after(inc.astype(BF16), mine), 'tm', [(0, 1)])  12.5 us
    ppermute x1, waiting for transfers between devices, body(): left = lax.ppermute(wide[..., 128:], ('x', 'c'), ring)  6.46 us
  transfers between devices with their start and end apart: 13, of which 8 were waited for; matrix products, arithmetic and copies ran while one was open for 2% of the time, Pallas kernels for 10%

profile of v1, /device:TPU:95, one launch (start us, length us, event | category | flops | bytes accessed | tf_op | source)
XLA Modules:
  0.0 180.8 jit_solution(12409818999877904332)
XLA Ops:
  6.5 0.0 copy-start.5
  6.5 0.0 all-gather.2.cloned.1.call-start
  6.5 1.2 copy.11
  7.7 0.8 copy.13
  8.5 0.0 all-gather.2.cloned.1.call-update
  8.5 0.0 copy-done.5
  8.6 2.0 %shard_map.73 = bf16[128,16,256]{2,1,0:T(8,128)(2,1)} custom-call(bf16[64,4,8,256]{3,2,1,0:T(8,128)(2,1)S(1)} %bitcast.26), custom_call_target="tpu_custom_call" | custom-call | tf_op jit(solution)/shard_map/pallas_call | solution.py:155
  10.5 0.0 copy-start.4
  10.5 14.9 %all-to-all-start = ((bf16[128,16,256]{2,1,0:T(8,128)(2,1)}), bf16[128,16,256]{2,1,0:T(8,128)(2,1)S(1)}, u32[]{:S(2)}, u32[]{:S(2)}) async-start(bf16[128,16,256]{2,1,0:T(8,128)(2,1)} %shard_map.73), calls=%async_computation | async-start | bytes 2097152 | tf_op jit(solution)/shard_map/all_to_all | solution.py:165
  25.4 0.0 copy-done.4
  25.4 0.3 collective-permute-start.6
  25.7 1.2 collective-permute-start.7
  26.9 1.2 collective-permute-start.8
  28.1 29.0 %all-to-all-done = bf16[128,16,256]{2,1,0:T(8,128)(2,1)S(1)} async-done(((bf16[128,16,256]{2,1,0:T(8,128)(2,1)}), bf16[128,16,256]{2,1,0:T(8,128)(2,1)S(1)}, u32[]{:S(2)}, u32[]{:S(2)}) %all-to-all-start) | async-done | bytes 1048608 | tf_op jit(solution)/shard_map/all_to_all | solution.py:165
  57.1 0.0 copy-start
  57.1 0.3 collective-permute-start.5
  57.4 2.8 %bitcast_convert_fusion.refs_0_ = bf16[64,4,8,256]{3,2,1,0:T(8,128)(2,1)} fusion(f32[64,1,4,8,256]{4,3,2,1,0:T(8,128)} %param.9), kind=kLoop, calls=%fused_computation.5 | loop fusion | flops 524288 | bytes 3145728 | tf_op jit(solution)/shard_map/convert_element_type | solution.py:174
  60.2 0.0 copy-done
  60.2 1.9 %collective-permute-start = (bf16[64,4,8,256]{3,2,1,0:T(8,128)(2,1)}, bf16[64,4,8,256]{3,2,1,0:T(8,128)(2,1)S(1)}, u32[]{:S(2)}, u32[]{:S(2)}) collective-permute-start(bf16[64,4,8,256]{3,2,1,0:T(8,128)(2,1)} %shard_map.74), channel_id=1, source_target_pairs={{0,128},{1,129},{2,130},{3,131},{4,132},{5,133},{6,134},{7,135},{8... | collective-permute-start | bytes 3145736 | tf_op jit(solution)/shard_map/ppermute | solution.py:174
  62.2 0.1 stack.27.refs_0_
  62.3 0.0 collective-permute-done.6.refs_4_
  62.3 0.0 collective-permute-done.7.refs_5_
  62.3 20.7 %collective-permute-done.8.refs_6_ = bf16[256,2048]{1,0:T(8,128)(2,1)} collective-permute-done((bf16[256,2048]{1,0:T(8,128)(2,1)S(1)}, bf16[256,2048]{1,0:T(8,128)(2,1)}, u32[]{:S(2)}, u32[]{:S(2)}) %collective-permute-start.8) | collective-permute-done | bytes 1048608 | tf_op jit(solution)/shard_map/ppermute | solution.py:150
  82.9 0.0 collective-permute-done.5.refs_2_
  82.9 0.0 copy-start.1
  82.9 1.2 copy-done.1
  84.2 4.6 %shard_map.76 = (bf16[4,2,256,128]{3,2,1,0:T(8,128)(2,1)S(1)}, bf16[4,2,256,128]{3,2,1,0:T(8,128)(2,1)S(1)}) custom-call(s32[6]{0:T(128)S(1)} %stack.27.refs_0_, bf16[16,8,16,256]{3,2,1,0:T(8,128)(2,1)S(1)} %bitcast.24, bf16[16,8,16,256]{3,2,1,0:T(8,128)(2,1)} %collective-permute-done.5.refs_2_, bf16[256,2048]{1,0:T(8,128)(2,1)S(1)} %copy-done.4, ...), custom_call_target="tpu_custom_call" | custom-call | tf_op jit(solution)/shard_map/pallas_call | solution.py:31
  88.8 0.1 collective-permute-start.9
  88.9 12.5 %collective-permute-done.refs_1_.refs_4_ = bf16[64,4,8,256]{3,2,1,0:T(8,128)(2,1)S(1)} collective-permute-done((bf16[64,4,8,256]{3,2,1,0:T(8,128)(2,1)}, bf16[64,4,8,256]{3,2,1,0:T(8,128)(2,1)S(1)}, u32[]{:S(2)}, u32[]{:S(2)}) %collective-permute-start) | collective-permute-done | bytes 1048608 | tf_op jit(solution)/shard_map/ppermute | solution.py:174
  101.4 0.1 collective-permute-done.9.refs_3_
  101.5 0.0 all-gather.2.cloned.1.call-done.refs_1_
  101.5 0.0 copy-start.3
  101.5 1.6 copy-done.3
  103.1 2.8 %shard_map.77 = bf16[64,64,128]{2,1,0:T(8,128)(2,1)} custom-call(s32[6]{0:T(128)S(1)} %stack.27.refs_0_, bf16[1024,1024]{1,0:T(8,128)(2,1)S(1)} %copy-done.3, bf16[4,2,256,128]{3,2,1,0:T(8,128)(2,1)S(1)} %get-tuple-element.7.refs_2_, bf16[4,2,256,128]{3,2,1,0:T(8,128)(2,1)S(1)} %collective-permute-done.9.refs_3_, ...), custom_call_target="tpu_custom_call" | custom-call | tf_op jit(solution)/shard_map/pallas_call | solution.py:31
  105.8 12.6 %all-to-all-start.1 = ((bf16[64,64,128]{2,1,0:T(8,128)(2,1)}), bf16[64,64,128]{2,1,0:T(8,128)(2,1)}, u32[]{:S(2)}, u32[]{:S(2)}) async-start(bf16[64,64,128]{2,1,0:T(8,128)(2,1)} %shard_map.77), calls=%async_computation.1 | async-start | bytes 2097152 | tf_op jit(solution)/shard_map/all_to_all | solution.py:202
  118.5 5.2 %collective-permute-start.1 = (bf16[2,4,8,256]{3,2,1,0:T(8,128)(2,1)S(1)}, bf16[2,4,8,256]{3,2,1,0:T(8,128)(2,1)S(1)}, u32[]{:S(2)}, u32[]{:S(2)}) collective-permute-start(bf16[2,4,8,256]{3,2,1,0:T(8,128)(2,1)S(1)} %get-tuple-element.12), channel_id=1, source_target_pairs={{0,8},{8,16},{16,24},{24,32},{32,40},{40,48},{48,56},{56,64},{64,7... | collective-permute-start | bytes 98312 | tf_op jit(solution)/shard_map/ppermute | solution.py:175
  123.7 1.9 %collective-permute-start.2 = (bf16[2,4,8,256]{3,2,1,0:T(8,128)(2,1)S(1)}, bf16[2,4,8,256]{3,2,1,0:T(8,128)(2,1)S(1)}, u32[]{:S(2)}, u32[]{:S(2)}) collective-permute-start(bf16[2,4,8,256]{3,2,1,0:T(8,128)(2,1)S(1)} %get-tuple-element.11), channel_id=1, source_target_pairs={{8,0},{16,8},{24,16},{32,24},{40,32},{48,40},{56,48},{64,56},{72,6... | collective-permute-start | bytes 98312 | tf_op jit(solution)/shard_map/ppermute | solution.py:176
  125.6 14.7 %collective-permute-done.1.refs_2_ = bf16[2,4,8,256]{3,2,1,0:T(8,128)(2,1)S(1)} collective-permute-done((bf16[2,4,8,256]{3,2,1,0:T(8,128)(2,1)S(1)}, bf16[2,4,8,256]{3,2,1,0:T(8,128)(2,1)S(1)}, u32[]{:S(2)}, u32[]{:S(2)}) %collective-permute-start.1) | collective-permute-done | bytes 32800 | tf_op jit(solution)/shard_map/ppermute | solution.py:175
  140.3 0.1 constant_dynamic-update-slice_fusion.1
  140.3 4.5 %collective-permute-done.2.refs_3_ = bf16[2,4,8,256]{3,2,1,0:T(8,128)(2,1)S(1)} collective-permute-done((bf16[2,4,8,256]{3,2,1,0:T(8,128)(2,1)S(1)}, bf16[2,4,8,256]{3,2,1,0:T(8,128)(2,1)S(1)}, u32[]{:S(2)}, u32[]{:S(2)}) %collective-permute-start.2) | collective-permute-done | bytes 32800 | tf_op jit(solution)/shard_map/ppermute | solution.py:176
  144.8 0.0 copy-start.6
  144.8 0.0 copy-start.7
  144.8 0.2 fusion
  145.0 2.4 %collective-permute-start.3 = (bf16[68,4,8,128]{3,2,1,0:T(8,128)(2,1)S(1)}, bf16[68,4,8,128]{3,2,1,0:T(8,128)(2,1)S(1)}, u32[]{:S(2)}, u32[]{:S(2)}) collective-permute-start(bf16[68,4,8,128]{3,2,1,0:T(8,128)(2,1)S(1)} %get-tuple-element.10), channel_id=1, source_target_pairs={{0,1},{1,2},{2,3},{3,4},{4,5},{5,6},{6,7},{7,0},{8,9},{9,10},{10,1... | collective-permute-start | bytes 1671176 | tf_op jit(solution)/shard_map/ppermute | solution.py:180
  147.4 0.0 collective-permute-start.4
  147.4 0.0 copy-done.6
  147.4 6.5 %collective-permute-done.3.refs_4_ = bf16[68,4,8,128]{3,2,1,0:T(8,128)(2,1)S(1)} collective-permute-done((bf16[68,4,8,128]{3,2,1,0:T(8,128)(2,1)S(1)}, bf16[68,4,8,128]{3,2,1,0:T(8,128)(2,1)S(1)}, u32[]{:S(2)}, u32[]{:S(2)}) %collective-permute-start.3) | collective-permute-done | bytes 557088 | tf_op jit(solution)/shard_map/ppermute | solution.py:180
  153.9 3.7 %collective-permute-done.4.refs_5_ = bf16[68,4,8,128]{3,2,1,0:T(8,128)(2,1)S(1)} collective-permute-done((bf16[68,4,8,128]{3,2,1,0:T(8,128)(2,1)S(1)}, bf16[68,4,8,128]{3,2,1,0:T(8,128)(2,1)S(1)}, u32[]{:S(2)}, u32[]{:S(2)}) %collective-permute-start.4) | collective-permute-done | bytes 557088 | tf_op jit(solution)/shard_map/ppermute | solution.py:181
  157.6 0.1 broadcast_in_dim.19.refs_6_
  157.7 0.1 broadcast_in_dim.21.refs_7_
  157.7 0.0 copy-done.7
  157.7 0.1 broadcast_in_dim.22.refs_8_
  157.8 10.6 %shard_map.75.base = f32[64,4,8,256]{3,2,1,0:T(8,128)S(1)} custom-call(f32[64,4,8,256]{3,2,1,0:T(8,128)} %bitcast.27, bf16[64,4,8,256]{3,2,1,0:T(8,128)(2,1)S(1)} %collective-permute-done.refs_1_.refs_4_, bf16[2,4,8,256]{3,2,1,0:T(8,128)(2,1)S(1)} %collective-permute-done.1.refs_2_, bf16[2,4,8,256]{3,2,1,0:T(8,128)(2,1)S(1)} %collective-permute-done.2.refs_3_, ...), custom_call_target="tpu_custom_call" | custom-call | bytes 30000000 | tf_op jit(solution)/shard_map/pallas_call | solution.py:31
  168.4 0.0 all-to-all-done.1.got
  168.4 0.0 copy-start.2
  168.4 1.6 copy-done.2
  170.0 3.9 %shard_map.78 = f32[64,4,8,256]{3,2,1,0:T(8,128)} custom-call(f32[64,4,8,256]{3,2,1,0:T(8,128)S(1)} %shard_map.75.base, f32[64,4,8,256]{3,2,1,0:T(8,128)S(1)} %bitcast.25, bf16[64,64,128]{2,1,0:T(8,128)(2,1)} %all-to-all-done.1.got), custom_call_target="tpu_custom_call" | custom-call | tf_op jit(solution)/shard_map/pallas_call | solution.py:205
  (6 shorter events, 0.0 us)
Async XLA Ops:
  6.5 2.0 %copy-start.5 = (bf16[64,1,4,8,256]{4,3,2,1,0:T(8,128)(2,1)S(1)}, bf16[64,1,4,8,256]{4,3,2,1,0:T(8,128)(2,1)}, u32[]{:S(2)}) copy-start(bf16[64,1,4,8,256]{4,3,2,1,0:T(8,128)(2,1)} %param.7) | copy-start | bytes 3145732
  6.5 94.9 %all-gather.2.cloned.1.call-start = ((), (), s32[]{:S(2)}) async-start(), calls=%async_computation.2 | async-start | bytes 2228224 | tf_op jit(solution)/shard_map/all_gather | solution.py:170
  10.5 14.9 %copy-start.4 = (bf16[256,2048]{1,0:T(8,128)(2,1)S(1)}, bf16[256,2048]{1,0:T(8,128)(2,1)}, u32[]{:S(2)}) copy-start(bf16[256,2048]{1,0:T(8,128)(2,1)} %refs_3_.1) | copy-start | bytes 3145732
  10.5 46.6 %all-to-all-start = ((bf16[128,16,256]{2,1,0:T(8,128)(2,1)}), bf16[128,16,256]{2,1,0:T(8,128)(2,1)S(1)}, u32[]{:S(2)}, u32[]{:S(2)}) async-start(bf16[128,16,256]{2,1,0:T(8,128)(2,1)} %shard_map.73), calls=%async_computation | async-start | bytes 2097152 | tf_op jit(solution)/shard_map/all_to_all | solution.py:165
  25.4 36.9 %collective-permute-start.6 = (bf16[256,2048]{1,0:T(8,128)(2,1)S(1)}, bf16[256,2048]{1,0:T(8,128)(2,1)}, u32[]{:S(2)}, u32[]{:S(2)}) collective-permute-start(bf16[256,2048]{1,0:T(8,128)(2,1)S(1)} %copy-done.4), channel_id=1, source_target_pairs={{0,2},{2,4},{4,6},{6,0},{1,3},{3,5},{5,7},{7,1},{8,10},{10,12},{12... | collective-permute-start | bytes 3145736 | tf_op jit(solution)/shard_map/ppermute | solution.py:150
  25.7 36.6 %collective-permute-start.7 = (bf16[256,2048]{1,0:T(8,128)(2,1)S(1)}, bf16[256,2048]{1,0:T(8,128)(2,1)}, u32[]{:S(2)}, u32[]{:S(2)}) collective-permute-start(bf16[256,2048]{1,0:T(8,128)(2,1)S(1)} %copy-done.4), channel_id=1, source_target_pairs={{0,6},{2,0},{4,2},{6,4},{1,7},{3,1},{5,3},{7,5},{8,14},{10,8},{12,... | collective-permute-start | bytes 3145736 | tf_op jit(solution)/shard_map/ppermute | solution.py:150
  26.9 56.0 %collective-permute-start.8 = (bf16[256,2048]{1,0:T(8,128)(2,1)S(1)}, bf16[256,2048]{1,0:T(8,128)(2,1)}, u32[]{:S(2)}, u32[]{:S(2)}) collective-permute-start(bf16[256,2048]{1,0:T(8,128)(2,1)S(1)} %copy-done.4), channel_id=1, source_target_pairs={{0,4},{2,6},{4,0},{6,2},{1,5},{3,7},{5,1},{7,3},{8,12},{10,14},{12... | collective-permute-start | bytes 3145736 | tf_op jit(solution)/shard_map/ppermute | solution.py:150
  57.1 3.1 %copy-start = (bf16[128,16,256]{2,1,0:T(8,128)(2,1)}, bf16[128,16,256]{2,1,0:T(8,128)(2,1)S(1)}, u32[]{:S(2)}) copy-start(bf16[128,16,256]{2,1,0:T(8,128)(2,1)S(1)} %all-to-all-done) | copy-start | bytes 3145732
  57.1 25.8 %collective-permute-start.5 = (bf16[16,8,16,256]{3,2,1,0:T(8,128)(2,1)S(1)}, bf16[16,8,16,256]{3,2,1,0:T(8,128)(2,1)}, u32[]{:S(2)}, u32[]{:S(2)}) collective-permute-start(bf16[16,8,16,256]{3,2,1,0:T(8,128)(2,1)S(1)} %bitcast.22), channel_id=1, source_target_pairs={{0,1},{1,0},{2,3},{3,2},{4,5},{5,4},{6,7},{7,6},{8,9},{9,8},{10,11... | collective-permute-start | bytes 3145736 | tf_op jit(solution)/shard_map/ppermute | solution.py:167
  60.2 41.2 %collective-permute-start = (bf16[64,4,8,256]{3,2,1,0:T(8,128)(2,1)}, bf16[64,4,8,256]{3,2,1,0:T(8,128)(2,1)S(1)}, u32[]{:S(2)}, u32[]{:S(2)}) collective-permute-start(bf16[64,4,8,256]{3,2,1,0:T(8,128)(2,1)} %shard_map.74), channel_id=1, source_target_pairs={{0,128},{1,129},{2,130},{3,131},{4,132},{5,133},{6,134},{7,135},{8... | collective-permute-start | bytes 3145736 | tf_op jit(solution)/shard_map/ppermute | solution.py:174
  82.9 1.2 copy-start.1
  88.8 12.7 %collective-permute-start.9 = (bf16[4,2,256,128]{3,2,1,0:T(8,128)(2,1)S(1)}, bf16[4,2,256,128]{3,2,1,0:T(8,128)(2,1)S(1)}, u32[]{:S(2)}, u32[]{:S(2)}) collective-permute-start(bf16[4,2,256,128]{3,2,1,0:T(8,128)(2,1)S(1)} %get-tuple-element.8), channel_id=1, source_target_pairs={{0,2},{2,0},{4,6},{6,4},{1,3},{3,1},{5,7},{7,5},{8,10},{10,8},{12,... | collective-permute-start | bytes 1572872 | tf_op jit(solution)/shard_map/ppermute | solution.py:198
  101.5 1.6 copy-start.3
  105.8 62.6 %all-to-all-start.1 = ((bf16[64,64,128]{2,1,0:T(8,128)(2,1)}), bf16[64,64,128]{2,1,0:T(8,128)(2,1)}, u32[]{:S(2)}, u32[]{:S(2)}) async-start(bf16[64,64,128]{2,1,0:T(8,128)(2,1)} %shard_map.77), calls=%async_computation.1 | async-start | bytes 2097152 | tf_op jit(solution)/shard_map/all_to_all | solution.py:202
  118.5 21.8 %collective-permute-start.1 = (bf16[2,4,8,256]{3,2,1,0:T(8,128)(2,1)S(1)}, bf16[2,4,8,256]{3,2,1,0:T(8,128)(2,1)S(1)}, u32[]{:S(2)}, u32[]{:S(2)}) collective-permute-start(bf16[2,4,8,256]{3,2,1,0:T(8,128)(2,1)S(1)} %get-tuple-element.12), channel_id=1, source_target_pairs={{0,8},{8,16},{16,24},{24,32},{32,40},{40,48},{48,56},{56,64},{64,7... | collective-permute-start | bytes 98312 | tf_op jit(solution)/shard_map/ppermute | solution.py:175
  123.7 21.1 %collective-permute-start.2 = (bf16[2,4,8,256]{3,2,1,0:T(8,128)(2,1)S(1)}, bf16[2,4,8,256]{3,2,1,0:T(8,128)(2,1)S(1)}, u32[]{:S(2)}, u32[]{:S(2)}) collective-permute-start(bf16[2,4,8,256]{3,2,1,0:T(8,128)(2,1)S(1)} %get-tuple-element.11), channel_id=1, source_target_pairs={{8,0},{16,8},{24,16},{32,24},{40,32},{48,40},{56,48},{64,56},{72,6... | collective-permute-start | bytes 98312 | tf_op jit(solution)/shard_map/ppermute | solution.py:176
  144.8 2.6 %copy-start.6 = (s32[2,8]{1,0:T(2,128)S(1)}, s32[2,8]{1,0:T(2,128)}, u32[]{:S(2)}) copy-start(s32[2,8]{1,0:T(2,128)} %param.12) | copy-start | bytes 196
  144.8 12.9 %copy-start.7 = (f32[4]{0:T(128)S(1)}, f32[4]{0:T(128)}, u32[]{:S(2)}) copy-start(f32[4]{0:T(128)} %param.13) | copy-start | bytes 52
  145.0 8.9 %collective-permute-start.3 = (bf16[68,4,8,128]{3,2,1,0:T(8,128)(2,1)S(1)}, bf16[68,4,8,128]{3,2,1,0:T(8,128)(2,1)S(1)}, u32[]{:S(2)}, u32[]{:S(2)}) collective-permute-start(bf16[68,4,8,128]{3,2,1,0:T(8,128)(2,1)S(1)} %get-tuple-element.10), channel_id=1, source_target_pairs={{0,1},{1,2},{2,3},{3,4},{4,5},{5,6},{6,7},{7,0},{8,9},{9,10},{10,1... | collective-permute-start | bytes 1671176 | tf_op jit(solution)/shard_map/ppermute | solution.py:180
  147.4 10.2 %collective-permute-start.4 = (bf16[68,4,8,128]{3,2,1,0:T(8,128)(2,1)S(1)}, bf16[68,4,8,128]{3,2,1,0:T(8,128)(2,1)S(1)}, u32[]{:S(2)}, u32[]{:S(2)}) collective-permute-start(bf16[68,4,8,128]{3,2,1,0:T(8,128)(2,1)S(1)} %get-tuple-element.9), channel_id=1, source_target_pairs={{1,0},{2,1},{3,2},{4,3},{5,4},{6,5},{7,6},{0,7},{9,8},{10,9},{11,1... | collective-permute-start | bytes 1671176 | tf_op jit(solution)/shard_map/ppermute | solution.py:181
  168.4 1.6 copy-start.2
Sparse Core Ops, SparseCore 0:
  9.8 82.1 all-gather.1

commit v2 on v1

v2 whole, which is shorter than its diff:
```python
import functools

import jax
import jax.numpy as jnp
from jax import lax
from jax.experimental import pallas as pl
from jax.experimental.pallas import tpu as pltpu
from jax.sharding import Mesh, PartitionSpec as P

F32, BF16 = jnp.float32, jnp.bfloat16
VMEM_LIMIT = 48 * 1024 * 1024
NT = (((1,), (1,)), ((), ()))


def call(kernel, out_shape, n_in, smem=(), scratch=(), before=(), work=0):
    def run(*refs):
        kernel(*refs[:n_in], *refs[n_in + len(before) :])

    in_specs = [
        pl.BlockSpec(memory_space=pltpu.SMEM if k in smem else pltpu.VMEM) for k in range(n_in)
    ] + [pl.BlockSpec(memory_space=pl.ANY)] * len(before)
    made = pl.pallas_call(
        run,
        out_shape=out_shape,
        in_specs=in_specs,
        out_specs=jax.tree.map(lambda _: pl.BlockSpec(memory_space=pltpu.VMEM), out_shape),
        scratch_shapes=list(scratch),
        compiler_params=pltpu.CompilerParams(vmem_limit_bytes=VMEM_LIMIT),
        cost_estimate=pl.CostEstimate(flops=0, bytes_accessed=work, transcendentals=0),
    )
    return lambda *args: made(*args, *before)


def after(value, *before):
    anywhere = pl.BlockSpec(memory_space=pl.ANY)
    return pl.pallas_call(
        lambda *refs: None,
        out_shape=jax.ShapeDtypeStruct(value.shape, value.dtype),
        in_specs=[anywhere] * (1 + len(before)),
        out_specs=anywhere,
        input_output_aliases={0: 0},
    )(value, *before)


def split_kernel(control, out, wide):
    for side in range(2):
        at = slice(side * 128, (side + 1) * 128)
        wide[side] = control[:, 0, :, at].astype(F32).reshape(512, 128)
    for level in range(8):
        for side in range(2):
            at = slice(side * 128, (side + 1) * 128)
            rows = wide[side, pl.ds(level, 64, stride=8), :].astype(BF16)
            out[level * 4 : (level + 1) * 4, :, at] = rows.reshape(4, 16, 128)


def smooth(rows, near, far):
    made = []
    for corr in (near, far):
        total = None
        for q in range(8):
            term = lax.dot_general(
                rows[:, q].reshape(256, 256),
                corr[:, q * 256 : (q + 1) * 256],
                NT,
                preferred_element_type=F32,
            )
            total = term if total is None else total + term
        made.append(total.astype(BF16))
    return made


def smooth_kernel(rows0, rows1, near, far, out):
    for k, rows in enumerate((rows0, rows1)):
        for tile, value in enumerate(smooth(rows, near, far)):
            out[k, tile] = value


def correlate_kernel(place, lat0, lat1, done, rows2, rows3, near, far, out, cols):
    for k in range(4):
        made = smooth((rows2, rows3)[k - 2], near, far) if k > 1 else (done[k, 0], done[k, 1])
        at = pl.ds(pl.multiple_of(place[1 + k] * 256, 256), 256)
        for tile, value in enumerate(made):
            cols[tile, at] = value
    for block in range(4):
        for tile in range(2):
            total = None
            for k, lat in enumerate((lat0, lat1)):
                at = pl.ds(pl.multiple_of(place[5 + k] * 512, 512), 512)
                left = lat[block * 256 : (block + 1) * 256]
                term = jnp.dot(left, cols[tile, at], preferred_element_type=F32)
                total = term if total is None else total + term
            total = total.astype(BF16)
            where = jnp.where(place[0] == 0, tile, 1 - tile)
            for k in range(4):
                out[(block * 4 + k) * 2 + where] = total[k * 64 : (k + 1) * 64]


def advect_kernel(inc, field, rim, off0, off1, courant, out, padded):
    step = pl.program_id(0)
    rows = inc.shape[0]

    @pl.when(step == 0)
    def _():
        def fill(a, _):
            padded[a, :, :, :256] = field[a].astype(F32)
            padded[a, :, :, 256:] = rim[a].astype(F32)
            return 0

        lax.fori_loop(0, 68, fill, 0, unroll=4)

    row_off = jnp.broadcast_to(off0[...][None], (4, 8, 384))
    col_off = jnp.broadcast_to(off1[...][None], (4, 8, 384))
    blend = courant[...]

    def one(k, _):
        a = step * rows + k
        at = padded[a + 2]
        moved = at
        for d in (-2, -1, 1, 2):
            moved = jnp.where(row_off == d, padded[a + 2 - d], moved)
        shifted = moved
        for d in (-2, -1, 1, 2):
            rolled = pltpu.roll(moved.reshape(32, 384), d % 384, 1).reshape(4, 8, 384)
            shifted = jnp.where(col_off == d, rolled, shifted)
        evolved = (1.0 - blend) * inc[k] + blend * shifted[:, :, :256]
        out[k] = evolved.astype(BF16)
        return 0

    lax.fori_loop(0, rows, one, 0, unroll=2)


def final_kernel(inc, past, dev, got, out, acc):
    rows = inc.shape[0]
    for v in range(4):
        for half in range(2):
            at = slice(half * 128, (half + 1) * 128)
            for level in range(8):
                row = got[v * 8 + level, :, at].astype(F32)
                acc[half, pl.ds(level, rows, stride=8), :] = row
            corr = acc[half].reshape(rows, 8, 128)
            rest = inc[:, v, :, at] - past[:, v, :, at].astype(F32)
            out[:, v, :, at] = rest - dev[:, v, :, at] * corr


def body(control, deviations, increments, lon_corr, lat_corr, offsets, courant):
    xh, xl, c = (lax.axis_index(name) for name in ("xh", "xl", "c"))
    swap = [(0, 1), (1, 0)]
    lats = ("zh", "y")
    params = pltpu.CompilerParams(vmem_limit_bytes=VMEM_LIMIT)
    free = pl.CostEstimate(flops=0, bytes_accessed=0, transcendentals=0)

    inc = increments.reshape(64, 4, 8, 256)

    across = lax.ppermute(lon_corr, "xh", swap)

    parts = pl.pallas_call(
        split_kernel,
        grid=(4,),
        out_shape=jax.ShapeDtypeStruct((128, 16, 256), BF16),
        in_specs=[pl.BlockSpec((64, 1, 8, 256), lambda v: (0, v, 0, 0))],
        out_specs=pl.BlockSpec((32, 16, 256), lambda v: (v, 0, 0)),
        scratch_shapes=[pltpu.VMEM((2, 512, 128), F32)],
        compiler_params=params,
        cost_estimate=free,
    )(control.reshape(64, 4, 8, 256))
    low = lax.ppermute(inc[62:].astype(BF16), lats, [(i, i + 1) for i in range(15)])
    high = lax.ppermute(inc[:2].astype(BF16), lats, [(i + 1, i) for i in range(15)])
    mine = lax.all_to_all(parts, ("zh", "y", "xh", "xl", "c"), 0, 0, tiled=True)
    wide = jnp.concatenate([low, inc.astype(BF16), high], axis=0)
    ring = [(i, (i + 1) % 8) for i in range(8)]
    back = [((i + 1) % 8, i) for i in range(8)]
    left = lax.ppermute(wide[..., 254:], ("xh", "xl", "c"), ring)
    right = lax.ppermute(wide[..., :2], ("xh", "xl", "c"), back)
    rim = jnp.concatenate([right, jnp.zeros((68, 4, 8, 124), BF16), left], axis=-1)
    off = jnp.broadcast_to(offsets[:, :, None], (2, 8, 384))
    big = pl.BlockSpec((16, 4, 8, 256), lambda i: (i, 0, 0, 0))
    evolved = pl.pallas_call(
        advect_kernel,
        grid=(4,),
        out_shape=jax.ShapeDtypeStruct((64, 4, 8, 256), BF16),
        in_specs=[big] + [pl.BlockSpec(memory_space=pltpu.VMEM)] * 5,
        out_specs=big,
        scratch_shapes=[pltpu.VMEM((68, 4, 8, 384), F32)],
        compiler_params=params,
        cost_estimate=pl.CostEstimate(flops=0, bytes_accessed=20_000_000, transcendentals=0),
    )(inc, wide, rim, off[0], off[1], jnp.broadcast_to(courant[:, None, None], (4, 8, 256)))

    mine = after(mine.reshape(16, 8, 16, 256), across, evolved)
    past = lax.ppermute(after(evolved, mine), "tm", [(0, 1)])
    paired = lax.ppermute(mine, "xl", swap)
    sibling = lax.ppermute(mine, "c", swap)
    opposite = lax.ppermute(paired, "c", swap)
    quarters = [xl * 2 + c, xl * 2 + 1 - c, 2 - 2 * xl + c, 3 - 2 * xl - c]
    place = jnp.stack([xh] + quarters + [c, 1 - c]).astype(jnp.int32)

    lat = lat_corr.reshape(64, 16, 4, 16).transpose(0, 2, 1, 3).reshape(64, 2, 512)
    lat = lax.dynamic_index_in_dim(lat, c, 1, keepdims=False)
    lat0 = lax.all_gather(lat, lats, axis=0, tiled=True)
    lat0 = after(lat0, paired)
    lat1 = lax.ppermute(lat0, "c", swap)

    dev = deviations.reshape(64, 4, 8, 256)
    made = jax.ShapeDtypeStruct((2, 2, 256, 256), BF16)
    done = call(smooth_kernel, made, 4, work=30_000_000)(mine, sibling, lon_corr, across)
    res = call(
        correlate_kernel,
        jax.ShapeDtypeStruct((32, 64, 256), BF16),
        8,
        smem=(0,),
        scratch=[pltpu.VMEM((2, 1024, 256), BF16)],
        before=(past,),
    )(place, lat0, lat1, done, paired, opposite, lon_corr, across)
    res = lax.all_to_all(res, ("zh", "y", "xh"), 0, 0, tiled=True)

    out = pl.pallas_call(
        final_kernel,
        grid=(4,),
        out_shape=jax.ShapeDtypeStruct((64, 4, 8, 256), F32),
        in_specs=[big, big, big, pl.BlockSpec((32, 16, 256), lambda i: (0, i, 0))],
        out_specs=big,
        scratch_shapes=[pltpu.VMEM((2, 128, 128), F32)],
        compiler_params=params,
        cost_estimate=free,
    )(inc, past, dev, res)
    return out.reshape(increments.shape)


def solution(mesh):
    fine = Mesh(mesh.devices.reshape(2, 4, 4, 2, 2, 2), ("tm", "zh", "y", "xh", "xl", "c"))
    lat, lon = ("zh", "y"), ("xh", "xl", "c")
    tile = P(lat, "tm", None, None, lon)
    in_specs = (tile, tile, tile, P(lon, None), P(lat, None), P(), P())
    return jax.shard_map(body, mesh=fine, in_specs=in_specs, out_specs=tile, check_vma=False)
```

time: 181 us -> 163 us (0.901)
  the two profiles are of different devices: /device:TPU:95 before, /device:TPU:32 now
where the time goes in v2:
time: 163 us
  blocking collectives  41.9 us (26%)
  waiting for transfers between devices  37.9 us (23%)
  starting transfers between devices  31.8 us (20%)
  Pallas kernels  19 us (12%)
  local copies, waits for them, and re-layouts  16.6 us (10%)
  between operations  13.6 us (8%)
  other arithmetic  2.08 us (1%)
    all_to_all x1, blocking collectives, body(): res = lax.all_to_all(res, ('zh', 'y', 'xh'), 0, 0, tiled=True)  41.9 us
    all_to_all x1, starting transfers between devices, body(): mine = lax.all_to_all(parts, ('zh', 'y', 'xh', 'xl', 'c'), 0, 0, tiled=True)  15 us
    ppermute x1, waiting for transfers between devices, body(): paired = lax.ppermute(mine, 'xl', swap)  14.3 us
    ppermute x1, waiting for transfers between devices, body(): left = lax.ppermute(wide[..., 254:], ('xh', 'xl', 'c'), ring)  10.6 us
    pallas_call x2, Pallas kernels, call(): return lambda *args: made(*args, *before)  7.85 us
    unnamed x28, local copies, waits for them, and re-layouts  6.36 us
    pallas_call x1, Pallas kernels, body(): pl.pallas_call(advect_kernel, grid=(4,), out_shape=jax.ShapeDtypeStruct((...  6.08 us
    all_gather x1, waiting for transfers between devices, body(): lat0 = lax.all_gather(lat, lats, axis=0, tiled=True)  5.76 us
  transfers between devices with their start and end apart: 12, of which 7 were waited for; matrix products, arithmetic and copies ran while one was open for 8% of the time, Pallas kernels for 5%

profile of v2, /device:TPU:32, one launch (start us, length us, event | category | flops | bytes accessed | tf_op | source)
XLA Modules:
  0.0 162.8 jit_solution(14908099508106267473)
XLA Ops:
  6.5 1.2 copy-done.9
  7.8 0.7 shard_map.74
  8.5 0.0 copy-start.8
  8.5 1.0 copy-done.8
  9.5 15.0 %all-to-all-start = ((bf16[128,16,256]{2,1,0:T(8,128)(2,1)}), bf16[128,16,256]{2,1,0:T(8,128)(2,1)S(1)}, u32[]{:S(2)}, u32[]{:S(2)}) async-start(bf16[128,16,256]{2,1,0:T(8,128)(2,1)} %copy-done.8), calls=%async_computation | async-start | bytes 2097152 | tf_op jit(solution)/shard_map/all_to_all | solution.py:168
  24.5 0.0 all-gather.3.cloned.1.call-start
  24.6 0.0 copy-done.10
  24.6 0.2 copy.23
  24.7 0.7 copy.24
  25.5 0.9 constant_dynamic-slice_fusion
  26.4 0.7 copy.27
  27.1 0.0 all-gather.3.cloned.1.call-update
  27.1 2.7 %collective-permute-start.4 = (bf16[256,2048]{1,0:T(8,128)(2,1)}, bf16[256,2048]{1,0:T(8,128)(2,1)}, u32[]{:S(2)}, u32[]{:S(2)}) collective-permute-start(bf16[256,2048]{1,0:T(8,128)(2,1)} %refs_6_.1), channel_id=1, source_target_pairs={{0,4},{4,0},{1,5},{5,1},{2,6},{6,2},{3,7},{7,3},{8,12},{12,8},{9,1... | collective-permute-start | bytes 3145736 | tf_op jit(solution)/shard_map/ppermute | solution.py:154
  29.9 0.0 copy-done
  29.9 0.3 bitcast_convert_fusion.1
  30.2 3.4 %collective-permute-start = (bf16[2,4,8,256]{3,2,1,0:T(8,128)(2,1)S(1)}, bf16[2,4,8,256]{3,2,1,0:T(8,128)(2,1)S(1)}, u32[]{:S(2)}, u32[]{:S(2)}) collective-permute-start(bf16[2,4,8,256]{3,2,1,0:T(8,128)(2,1)S(1)} %get-tuple-element.9), channel_id=1, source_target_pairs={{0,8},{8,16},{16,24},{24,32},{32,40},{40,48},{48,56},{56,64},{64,7... | collective-permute-start | bytes 98312 | tf_op jit(solution)/shard_map/ppermute | solution.py:166
  33.5 1.3 collective-permute-start.1
  34.8 0.3 collective-permute-done
  35.1 4.5 %collective-permute-done.1 = bf16[2,4,8,256]{3,2,1,0:T(8,128)(2,1)S(1)} collective-permute-done((bf16[2,4,8,256]{3,2,1,0:T(8,128)(2,1)S(1)}, bf16[2,4,8,256]{3,2,1,0:T(8,128)(2,1)S(1)}, u32[]{:S(2)}, u32[]{:S(2)}) %collective-permute-start.1) | collective-permute-done | bytes 32800 | tf_op jit(solution)/shard_map/ppermute | solution.py:167
  39.6 0.1 pad_maximum_fusion.field
  39.7 0.0 copy-start.3
  39.7 1.3 fusion
  41.1 0.0 copy-done.3
  41.1 1.7 %copy.19 = bf16[68,4,8,2]{0,2,3,1:T(8,128)(2,1)S(1)} copy(bf16[68,4,8,2]{3,2,1,0:T(8,128)(2,1)} %get-tuple-element.7) | data formatting | bytes 17408 | tf_op jit(solution)/shard_map/slice | solution.py:173
  42.8 1.7 %copy.20 = bf16[68,4,8,2]{0,2,3,1:T(8,128)(2,1)S(1)} copy(bf16[68,4,8,2]{3,2,1,0:T(8,128)(2,1)} %get-tuple-element.8) | data formatting | bytes 17408 | tf_op jit(solution)/shard_map/slice | solution.py:172
  44.5 0.0 collective-permute-start.3
  44.5 3.0 %collective-permute-start.2 = (bf16[68,4,8,2]{0,2,3,1:T(8,128)(2,1)S(1)}, bf16[68,4,8,2]{0,2,3,1:T(8,128)(2,1)S(1)}, u32[]{:S(2)}, u32[]{:S(2)}) collective-permute-start(bf16[68,4,8,2]{0,2,3,1:T(8,128)(2,1)S(1)} %copy.19), channel_id=1, source_target_pairs={{1,0},{2,1},{3,2},{4,3},{5,4},{6,5},{7,6},{0,7},{9,8},{10,9},{11,1... | collective-permute-start | bytes 26120 | tf_op jit(solution)/shard_map/ppermute | solution.py:173
  47.4 0.0 copy-done.11
  47.4 0.1 pad.1.clone
  47.5 1.4 collective-permute-done.2
  48.9 1.7 %copy.21 = bf16[68,4,8,2]{3,2,1,0:T(8,128)(2,1)} copy(bf16[68,4,8,2]{0,2,3,1:T(8,128)(2,1)S(1)} %collective-permute-done.2) | data formatting | bytes 17408 | tf_op jit(solution)/shard_map/ppermute | solution.py:173
  50.6 10.6 %collective-permute-done.3 = bf16[68,4,8,2]{0,2,3,1:T(8,128)(2,1)S(1)} collective-permute-done((bf16[68,4,8,2]{0,2,3,1:T(8,128)(2,1)S(1)}, bf16[68,4,8,2]{0,2,3,1:T(8,128)(2,1)S(1)}, u32[]{:S(2)}, u32[]{:S(2)}) %collective-permute-start.3) | collective-permute-done | bytes 8736 | tf_op jit(solution)/shard_map/ppermute | solution.py:172
  61.2 1.7 %copy.22 = bf16[68,4,8,2]{3,2,1,0:T(8,128)(2,1)} copy(bf16[68,4,8,2]{0,2,3,1:T(8,128)(2,1)S(1)} %collective-permute-done.3) | data formatting | bytes 17408 | tf_op jit(solution)/shard_map/ppermute | solution.py:172
  62.9 1.7 %pad_maximum_fusion.1.rim = bf16[68,4,8,128]{3,2,1,0:T(8,128)(2,1)S(1)} fusion(bf16[68,4,8,2]{3,2,1,0:T(8,128)(2,1)} %copy.22, bf16[68,4,8,2]{3,2,1,0:T(8,128)(2,1)} %copy.21, bf16[128]{0:T(256)(128)(2,1)S(1)} %pad.1.clone), kind=kLoop, calls=%fused_computation.2 | loop fusion | flops 1671168 | bytes 574720 | tf_op jit(solution)/shard_map/concatenate | solution.py:174
  64.6 0.1 broadcast_in_dim.25.off1
  64.7 0.1 broadcast_in_dim.23.off0
  64.7 0.0 copy-done.12
  64.7 0.1 broadcast_in_dim.26.courant
  64.8 0.0 copy-done.4
  64.8 6.1 %shard_map.73.refs_2_.refs_0_ = bf16[64,4,8,256]{3,2,1,0:T(8,128)(2,1)S(1)} custom-call(f32[64,4,8,256]{3,2,1,0:T(8,128)S(1)} %bitcast.30, bf16[68,4,8,256]{3,2,1,0:T(8,128)(2,1)S(1)} %copy-done.4, bf16[68,4,8,128]{3,2,1,0:T(8,128)(2,1)S(1)} %pad_maximum_fusion.1.rim, s32[8,384]{1,0:T(8,128)S(1)} %broadcast_in_dim.23.off0, ...), custom_call_target="tpu_custom_call" | custom-call | bytes 20000000 | tf_op jit(solution)/shard_map/pallas_call | solution.py:177
  70.9 0.0 copy-start.5
  70.9 1.0 copy-done.5
  71.9 0.0 collective-permute-done.4.refs_1_.refs_3_.refs_7_
  71.9 0.0 all-to-all-done
  71.9 1.0 copy-done.1
  72.9 1.7 %collective-permute-start.6 = (bf16[16,8,16,256]{3,2,1,0:T(8,128)(2,1)}, bf16[16,8,16,256]{3,2,1,0:T(8,128)(2,1)}, u32[]{:S(2)}, u32[]{:S(2)}) collective-permute-start(bf16[16,8,16,256]{3,2,1,0:T(8,128)(2,1)} %shard_map.75.refs_1_.refs_0_), channel_id=1, source_target_pairs={{0,2},{2,0},{1,3},{3,1},{4,6},{6,4},{5,7},{7,5},{8,10},{10,8},{9,1... | collective-permute-start | bytes 3145736 | tf_op jit(solution)/shard_map/ppermute | solution.py:190
  74.5 0.0 copy-done.2
  74.5 1.9 %collective-permute-start.8 = (bf16[16,8,16,256]{3,2,1,0:T(8,128)(2,1)S(1)}, bf16[16,8,16,256]{3,2,1,0:T(8,128)(2,1)}, u32[]{:S(2)}, u32[]{:S(2)}) collective-permute-start(bf16[16,8,16,256]{3,2,1,0:T(8,128)(2,1)S(1)} %copy-done.2), channel_id=1, source_target_pairs={{0,1},{1,0},{2,3},{3,2},{4,5},{5,4},{6,7},{7,6},{8,9},{9,8},{10,11... | collective-permute-start | bytes 3145736 | tf_op jit(solution)/shard_map/ppermute | solution.py:191
  76.4 1.3 collective-permute-start.5
  77.7 5.8 %all-gather.3.cloned.1.call-done = bf16[1024,1,512]{2,0,1:T(8,128)(2,1)} async-done(((bf16[64,1,512]{2,0,1:T(8,128)(2,1)}), bf16[1024,1,512]{2,0,1:T(8,128)(2,1)}) %all-gather.3.cloned.1.call-update) | async-done | bytes 1048592 | tf_op jit(solution)/shard_map/all_gather | solution.py:198
  83.5 14.3 %collective-permute-done.6.refs_1_.refs_4_ = bf16[16,8,16,256]{3,2,1,0:T(8,128)(2,1)} collective-permute-done((bf16[16,8,16,256]{3,2,1,0:T(8,128)(2,1)}, bf16[16,8,16,256]{3,2,1,0:T(8,128)(2,1)}, u32[]{:S(2)}, u32[]{:S(2)}) %collective-permute-start.6) | collective-permute-done | bytes 1048608 | tf_op jit(solution)/shard_map/ppermute | solution.py:190
  97.8 1.6 collective-permute-start.7
  99.3 0.0 collective-permute-start.9
  99.3 0.1 stack.31.refs_0_
  99.4 0.0 collective-permute-done.8.refs_1_
  99.4 0.0 copy-start.7
  99.4 1.3 copy-done.7
  100.7 2.8 %shard_map.78.refs_3_ = bf16[2,2,256,256]{3,2,1,0:T(8,128)(2,1)S(1)} custom-call(bf16[16,8,16,256]{3,2,1,0:T(8,128)(2,1)S(1)} %copy-done.2, bf16[16,8,16,256]{3,2,1,0:T(8,128)(2,1)} %collective-permute-done.8.refs_1_, bf16[256,2048]{1,0:T(8,128)(2,1)S(1)} %copy-done.7, bf16[256,2048]{1,0:T(8,128)(2,1)} %collective-permute-done.4.refs_1_.refs_3_.refs_7_), custom_call_target="tpu_custom_call" | custom-call | bytes 30000000 | tf_op jit(solution)/shard_map/pallas_call | solution.py:31
  103.6 1.1 collective-permute-done.5.refs_8_.past
  104.7 0.0 collective-permute-done.7.refs_2_
  104.7 0.0 collective-permute-done.9.refs_5_
  104.7 5.0 %shard_map.79 = bf16[32,64,256]{2,1,0:T(8,128)(2,1)S(1)} custom-call(s32[7]{0:T(128)S(1)} %stack.31.refs_0_, bf16[1024,512]{1,0:T(8,128)(2,1)S(1)} %copy-done.6, bf16[1024,512]{1,0:T(8,128)(2,1)} %collective-permute-done.7.refs_2_, bf16[2,2,256,256]{3,2,1,0:T(8,128)(2,1)S(1)} %shard_map.78.refs_3_, ...), custom_call_target="tpu_custom_call" | custom-call | tf_op jit(solution)/shard_map/pallas_call | solution.py:31
  109.7 41.9 %all_to_all.10.got = bf16[32,64,256]{2,1,0:T(8,128)(2,1)S(1)} all-to-all(bf16[32,64,256]{2,1,0:T(8,128)(2,1)S(1)} %shard_map.79), channel_id=1, replica_groups=mesh['tm'=2,'zh'=4,'y'=4,'xh'=2,'xl'=2,'c'=2] {'zh','y','xh'}, dimensions={0} | all-to-all | bytes 2097152 | tf_op jit(solution)/shard_map/all_to_all | solution.py:213
  151.6 4.3 %shard_map.80 = f32[64,4,8,256]{3,2,1,0:T(8,128)} custom-call(f32[64,4,8,256]{3,2,1,0:T(8,128)S(1)} %bitcast.31, bf16[64,4,8,256]{3,2,1,0:T(8,128)(2,1)} %collective-permute-done.5.refs_8_.past, f32[64,4,8,256]{3,2,1,0:T(8,128)} %bitcast.35, bf16[32,64,256]{2,1,0:T(8,128)(2,1)S(1)} %all_to_all.10.got), custom_call_target="tpu_custom_call" | custom-call | tf_op jit(solution)/shard_map/pallas_call | solution.py:215
  (16 shorter events, 0.0 us)
Async XLA Ops:
  6.5 1.2 copy-start.9
  7.8 16.8 %copy-start.10 = (bf16[64,1024]{1,0:T(8,128)(2,1)S(1)}, bf16[64,1024]{1,0:T(8,128)(2,1)}, u32[]{:S(2)}) copy-start(bf16[64,1024]{1,0:T(8,128)(2,1)} %param.11) | copy-start | bytes 393220
  8.5 1.0 copy-start.8
  9.5 20.4 %copy-start = (f32[64,1,4,8,256]{4,3,2,1,0:T(8,128)S(1)}, f32[64,1,4,8,256]{4,3,2,1,0:T(8,128)}, u32[]{:S(2)}) copy-start(f32[64,1,4,8,256]{4,3,2,1,0:T(8,128)} %param.9) | copy-start | bytes 6291460
  9.5 62.4 %all-to-all-start = ((bf16[128,16,256]{2,1,0:T(8,128)(2,1)}), bf16[128,16,256]{2,1,0:T(8,128)(2,1)S(1)}, u32[]{:S(2)}, u32[]{:S(2)}) async-start(bf16[128,16,256]{2,1,0:T(8,128)(2,1)} %copy-done.8), calls=%async_computation | async-start | bytes 2097152 | tf_op jit(solution)/shard_map/all_to_all | solution.py:168
  24.5 59.0 %all-gather.3.cloned.1.call-start = ((), (), s32[]{:S(2)}) async-start(), calls=%async_computation.2 | async-start | bytes 1114112 | tf_op jit(solution)/shard_map/all_gather | solution.py:198
  27.1 44.7 %collective-permute-start.4 = (bf16[256,2048]{1,0:T(8,128)(2,1)}, bf16[256,2048]{1,0:T(8,128)(2,1)}, u32[]{:S(2)}, u32[]{:S(2)}) collective-permute-start(bf16[256,2048]{1,0:T(8,128)(2,1)} %refs_6_.1), channel_id=1, source_target_pairs={{0,4},{4,0},{1,5},{5,1},{2,6},{6,2},{3,7},{7,3},{8,12},{12,8},{9,1... | collective-permute-start | bytes 3145736 | tf_op jit(solution)/shard_map/ppermute | solution.py:154
  30.2 5.0 %collective-permute-start = (bf16[2,4,8,256]{3,2,1,0:T(8,128)(2,1)S(1)}, bf16[2,4,8,256]{3,2,1,0:T(8,128)(2,1)S(1)}, u32[]{:S(2)}, u32[]{:S(2)}) collective-permute-start(bf16[2,4,8,256]{3,2,1,0:T(8,128)(2,1)S(1)} %get-tuple-element.9), channel_id=1, source_target_pairs={{0,8},{8,16},{16,24},{24,32},{32,40},{40,48},{48,56},{56,64},{64,7... | collective-permute-start | bytes 98312 | tf_op jit(solution)/shard_map/ppermute | solution.py:166
  33.5 6.0 %collective-permute-start.1 = (bf16[2,4,8,256]{3,2,1,0:T(8,128)(2,1)S(1)}, bf16[2,4,8,256]{3,2,1,0:T(8,128)(2,1)S(1)}, u32[]{:S(2)}, u32[]{:S(2)}) collective-permute-start(bf16[2,4,8,256]{3,2,1,0:T(8,128)(2,1)S(1)} %get-tuple-element.10), channel_id=1, source_target_pairs={{8,0},{16,8},{24,16},{32,24},{40,32},{48,40},{56,48},{64,56},{72,6... | collective-permute-start | bytes 98312 | tf_op jit(solution)/shard_map/ppermute | solution.py:167
  39.7 1.4 copy-start.3
  41.1 6.4 %copy-start.11 = (s32[2,8]{1,0:T(2,128)S(1)}, s32[2,8]{1,0:T(2,128)}, u32[]{:S(2)}) copy-start(s32[2,8]{1,0:T(2,128)} %param.12) | copy-start | bytes 196
  44.5 16.7 %collective-permute-start.3 = (bf16[68,4,8,2]{0,2,3,1:T(8,128)(2,1)S(1)}, bf16[68,4,8,2]{0,2,3,1:T(8,128)(2,1)S(1)}, u32[]{:S(2)}, u32[]{:S(2)}) collective-permute-start(bf16[68,4,8,2]{0,2,3,1:T(8,128)(2,1)S(1)} %copy.20), channel_id=1, source_target_pairs={{0,1},{1,2},{2,3},{3,4},{4,5},{5,6},{6,7},{7,0},{8,9},{9,10},{10,1... | collective-permute-start | bytes 26120 | tf_op jit(solution)/shard_map/ppermute | solution.py:172
  44.5 4.4 %collective-permute-start.2 = (bf16[68,4,8,2]{0,2,3,1:T(8,128)(2,1)S(1)}, bf16[68,4,8,2]{0,2,3,1:T(8,128)(2,1)S(1)}, u32[]{:S(2)}, u32[]{:S(2)}) collective-permute-start(bf16[68,4,8,2]{0,2,3,1:T(8,128)(2,1)S(1)} %copy.19), channel_id=1, source_target_pairs={{1,0},{2,1},{3,2},{4,3},{5,4},{6,5},{7,6},{0,7},{9,8},{10,9},{11,1... | collective-permute-start | bytes 26120 | tf_op jit(solution)/shard_map/ppermute | solution.py:173
  50.6 14.1 %copy-start.12 = (f32[4]{0:T(128)S(1)}, f32[4]{0:T(128)}, u32[]{:S(2)}) copy-start(f32[4]{0:T(128)} %param.13) | copy-start | bytes 52
  62.9 1.9 %copy-start.4 = (bf16[68,4,8,256]{3,2,1,0:T(8,128)(2,1)S(1)}, bf16[68,4,8,256]{3,2,1,0:T(8,128)(2,1)}, u32[]{:S(2)}) copy-start(bf16[68,4,8,256]{3,2,1,0:T(8,128)(2,1)} %copy-done.3) | copy-start | bytes 3342340
  70.9 1.0 copy-start.5
  71.9 1.0 copy-start.1
  72.9 1.7 %copy-start.2 = (bf16[16,8,16,256]{3,2,1,0:T(8,128)(2,1)S(1)}, bf16[16,8,16,256]{3,2,1,0:T(8,128)(2,1)}, u32[]{:S(2)}) copy-start(bf16[16,8,16,256]{3,2,1,0:T(8,128)(2,1)} %shard_map.75.refs_1_.refs_0_) | copy-start | bytes 3145732
  72.9 24.9 %collective-permute-start.6 = (bf16[16,8,16,256]{3,2,1,0:T(8,128)(2,1)}, bf16[16,8,16,256]{3,2,1,0:T(8,128)(2,1)}, u32[]{:S(2)}, u32[]{:S(2)}) collective-permute-start(bf16[16,8,16,256]{3,2,1,0:T(8,128)(2,1)} %shard_map.75.refs_1_.refs_0_), channel_id=1, source_target_pairs={{0,2},{2,0},{1,3},{3,1},{4,6},{6,4},{5,7},{7,5},{8,10},{10,8},{9,1... | collective-permute-start | bytes 3145736 | tf_op jit(solution)/shard_map/ppermute | solution.py:190
  74.5 24.9 %collective-permute-start.8 = (bf16[16,8,16,256]{3,2,1,0:T(8,128)(2,1)S(1)}, bf16[16,8,16,256]{3,2,1,0:T(8,128)(2,1)}, u32[]{:S(2)}, u32[]{:S(2)}) collective-permute-start(bf16[16,8,16,256]{3,2,1,0:T(8,128)(2,1)S(1)} %copy-done.2), channel_id=1, source_target_pairs={{0,1},{1,0},{2,3},{3,2},{4,5},{5,4},{6,7},{7,6},{8,9},{9,8},{10,11... | collective-permute-start | bytes 3145736 | tf_op jit(solution)/shard_map/ppermute | solution.py:191
  76.4 28.2 %collective-permute-start.5 = (bf16[64,4,8,256]{3,2,1,0:T(8,128)(2,1)}, bf16[64,4,8,256]{3,2,1,0:T(8,128)(2,1)}, u32[]{:S(2)}, u32[]{:S(2)}) collective-permute-start(bf16[64,4,8,256]{3,2,1,0:T(8,128)(2,1)} %shard_map.76), channel_id=1, source_target_pairs={{0,128},{1,129},{2,130},{3,131},{4,132},{5,133},{6,134},{7,135},{8... | collective-permute-start | bytes 3145736 | tf_op jit(solution)/shard_map/ppermute | solution.py:189
  97.8 6.9 %collective-permute-start.7 = (bf16[1024,512]{1,0:T(8,128)(2,1)}, bf16[1024,512]{1,0:T(8,128)(2,1)}, u32[]{:S(2)}, u32[]{:S(2)}) collective-permute-start(bf16[1024,512]{1,0:T(8,128)(2,1)} %shard_map.77.refs_1_), channel_id=1, source_target_pairs={{0,1},{1,0},{2,3},{3,2},{4,5},{5,4},{6,7},{7,6},{8,9},{9,8},{10,11... | collective-permute-start | bytes 3145736 | tf_op jit(solution)/shard_map/ppermute | solution.py:200
  99.3 5.4 %collective-permute-start.9 = (bf16[16,8,16,256]{3,2,1,0:T(8,128)(2,1)}, bf16[16,8,16,256]{3,2,1,0:T(8,128)(2,1)}, u32[]{:S(2)}, u32[]{:S(2)}) collective-permute-start(bf16[16,8,16,256]{3,2,1,0:T(8,128)(2,1)} %collective-permute-done.6.refs_1_.refs_4_), channel_id=1, source_target_pairs={{0,1},{1,0},{2,3},{3,2},{4,5},{5,4},{6,7},{7,6},{8,9},{9,8},{10,11... | collective-permute-start | bytes 3145736 | tf_op jit(solution)/shard_map/ppermute | solution.py:192
  99.4 5.3 %copy-start.6 = (bf16[1024,512]{1,0:T(8,128)(2,1)S(1)}, bf16[1024,512]{1,0:T(8,128)(2,1)}, u32[]{:S(2)}) copy-start(bf16[1024,512]{1,0:T(8,128)(2,1)} %shard_map.77.refs_1_) | copy-start | bytes 3145732
  99.4 1.3 copy-start.7
Sparse Core Ops, SparseCore 0:
  27.8 55.6 all-gather.2

commit v3 on v2

--- a/solution.py
+++ b/solution.py
@@ -49,38 +49,36 @@
     for level in range(8):
         for side in range(2):
             at = slice(side * 128, (side + 1) * 128)
-            rows = wide[side, pl.ds(level, 64, stride=8), :].astype(BF16)
-            out[level * 4 : (level + 1) * 4, :, at] = rows.reshape(4, 16, 128)
-
-
-def smooth(rows, near, far):
-    made = []
-    for corr in (near, far):
-        total = None
-        for q in range(8):
+            out[level, :, at] = wide[side, pl.ds(level, 64, stride=8), :].astype(BF16)
+
+
+def smooth(starts, pieces, corr, block):
+    total = None
+    for start, piece in zip(starts, pieces):
+        for k in range(2):
             term = lax.dot_general(
-                rows[:, q].reshape(256, 256),
-                corr[:, q * 256 : (q + 1) * 256],
+                piece[block * 4 : (block + 1) * 4, k].reshape(256, 256),
+                corr[:, pl.ds(pl.multiple_of(start + k * 512, 256), 256)],
                 NT,
                 preferred_element_type=F32,
             )
             total = term if total is None else total + term
-        made.append(total.astype(BF16))
-    return made
-
-
-def smooth_kernel(rows0, rows1, near, far, out):
-    for k, rows in enumerate((rows0, rows1)):
-        for tile, value in enumerate(smooth(rows, near, far)):
-            out[k, tile] = value
-
-
-def correlate_kernel(place, lat0, lat1, done, rows2, rows3, near, far, out, cols):
-    for k in range(4):
-        made = smooth((rows2, rows3)[k - 2], near, far) if k > 1 else (done[k, 0], done[k, 1])
-        at = pl.ds(pl.multiple_of(place[1 + k] * 256, 256), 256)
-        for tile, value in enumerate(made):
-            cols[tile, at] = value
+    return total
+
+
+def smooth_kernel(place, rows0, rows1, near, far, out):
+    for tile, corr in enumerate((near, far)):
+        for block in range(4):
+            at = slice(block * 256, (block + 1) * 256)
+            out[tile, at] = smooth((place[1], place[2]), (rows0, rows1), corr, block)
+
+
+def correlate_kernel(place, lat0, lat1, begun, rows2, rows3, near, far, out, cols):
+    for tile, corr in enumerate((near, far)):
+        for block in range(4):
+            at = slice(block * 256, (block + 1) * 256)
+            rest = smooth((place[3], place[4]), (rows2, rows3), corr, block)
+            cols[tile, at] = (begun[tile, at] + rest).astype(BF16)
     for block in range(4):
         for tile in range(2):
             total = None
@@ -122,24 +120,23 @@
         for d in (-2, -1, 1, 2):
             rolled = pltpu.roll(moved.reshape(32, 384), d % 384, 1).reshape(4, 8, 384)
             shifted = jnp.where(col_off == d, rolled, shifted)
-        evolved = (1.0 - blend) * inc[k] + blend * shifted[:, :, :256]
-        out[k] = evolved.astype(BF16)
+        evolved = (1.0 - blend) * at[:, :, :256] + blend * shifted[:, :, :256]
+        out[k] = inc[k] - evolved
         return 0
 
     lax.fori_loop(0, rows, one, 0, unroll=2)
 
 
-def final_kernel(inc, past, dev, got, out, acc):
-    rows = inc.shape[0]
+def final_kernel(turned, base, dev, got, out, acc):
+    rows = base.shape[0]
     for v in range(4):
         for half in range(2):
             at = slice(half * 128, (half + 1) * 128)
             for level in range(8):
-                row = got[v * 8 + level, :, at].astype(F32)
+                row = got[v * 8 + jnp.bitwise_xor(level, turned[0]), :, at].astype(F32)
                 acc[half, pl.ds(level, rows, stride=8), :] = row
             corr = acc[half].reshape(rows, 8, 128)
-            rest = inc[:, v, :, at] - past[:, v, :, at].astype(F32)
-            out[:, v, :, at] = rest - dev[:, v, :, at] * corr
+            out[:, v, :, at] = base[:, v, :, at] - dev[:, v, :, at] * corr
 
 
 def body(control, deviations, increments, lon_corr, lat_corr, offsets, courant):
@@ -151,22 +148,38 @@
 
     inc = increments.reshape(64, 4, 8, 256)
 
-    across = lax.ppermute(lon_corr, "xh", swap)
-
+    across = lax.ppermute(lon_corr, ("xh", "xl"), [(i, 3 - i) for i in range(4)])
+
+    lat = lax.dynamic_slice_in_dim(lat_corr, c * 512, 512, 1)
     parts = pl.pallas_call(
-        split_kernel,
+        lambda control, lat, out, wide: split_kernel(control, out, wide),
         grid=(4,),
-        out_shape=jax.ShapeDtypeStruct((128, 16, 256), BF16),
-        in_specs=[pl.BlockSpec((64, 1, 8, 256), lambda v: (0, v, 0, 0))],
-        out_specs=pl.BlockSpec((32, 16, 256), lambda v: (v, 0, 0)),
+        out_shape=jax.ShapeDtypeStruct((32, 64, 256), BF16),
+        in_specs=[
+            pl.BlockSpec((64, 1, 8, 256), lambda v: (0, v, 0, 0)),
+            pl.BlockSpec(memory_space=pl.ANY),
+        ],
+        out_specs=pl.BlockSpec((8, 64, 256), lambda v: (v, 0, 0)),
         scratch_shapes=[pltpu.VMEM((2, 512, 128), F32)],
         compiler_params=params,
         cost_estimate=free,
-    )(control.reshape(64, 4, 8, 256))
+    )(control.reshape(64, 4, 8, 256), lat)
     low = lax.ppermute(inc[62:].astype(BF16), lats, [(i, i + 1) for i in range(15)])
     high = lax.ppermute(inc[:2].astype(BF16), lats, [(i + 1, i) for i in range(15)])
-    mine = lax.all_to_all(parts, ("zh", "y", "xh", "xl", "c"), 0, 0, tiled=True)
+    mine = lax.all_to_all(parts, ("zh", "y", "xl"), 0, 0, tiled=True)
+    mine = after(mine.reshape(16, 2, 64, 256), across, low, high)
+    paired = lax.ppermute(mine, "xh", swap)
+    sibling = lax.ppermute(mine, "c", swap)
+    opposite = lax.ppermute(paired, "c", swap)
+    starts = [(a * 4 + b) * 256 for a in (xh, 1 - xh) for b in (c, 1 - c)]
+    place = jnp.stack([xh] + starts + [c, 1 - c]).astype(jnp.int32)
+
+    lat0 = after(lax.all_gather(lat, lats, axis=0, tiled=True), paired)
+    lat1 = lax.ppermute(lat0, "c", swap)
+
+    dev = deviations.reshape(64, 4, 8, 256)
     wide = jnp.concatenate([low, inc.astype(BF16), high], axis=0)
+    wide = lax.ppermute(wide, "tm", [(0, 1)])
     ring = [(i, (i + 1) % 8) for i in range(8)]
     back = [((i + 1) % 8, i) for i in range(8)]
     left = lax.ppermute(wide[..., 254:], ("xh", "xl", "c"), ring)
@@ -174,10 +187,10 @@
     rim = jnp.concatenate([right, jnp.zeros((68, 4, 8, 124), BF16), left], axis=-1)
     off = jnp.broadcast_to(offsets[:, :, None], (2, 8, 384))
     big = pl.BlockSpec((16, 4, 8, 256), lambda i: (i, 0, 0, 0))
-    evolved = pl.pallas_call(
+    base = pl.pallas_call(
         advect_kernel,
         grid=(4,),
-        out_shape=jax.ShapeDtypeStruct((64, 4, 8, 256), BF16),
+        out_shape=jax.ShapeDtypeStruct((64, 4, 8, 256), F32),
         in_specs=[big] + [pl.BlockSpec(memory_space=pltpu.VMEM)] * 5,
         out_specs=big,
         scratch_shapes=[pltpu.VMEM((68, 4, 8, 384), F32)],
@@ -185,43 +198,34 @@
         cost_estimate=pl.CostEstimate(flops=0, bytes_accessed=20_000_000, transcendentals=0),
     )(inc, wide, rim, off[0], off[1], jnp.broadcast_to(courant[:, None, None], (4, 8, 256)))
 
-    mine = after(mine.reshape(16, 8, 16, 256), across, evolved)
-    past = lax.ppermute(after(evolved, mine), "tm", [(0, 1)])
-    paired = lax.ppermute(mine, "xl", swap)
-    sibling = lax.ppermute(mine, "c", swap)
-    opposite = lax.ppermute(paired, "c", swap)
-    quarters = [xl * 2 + c, xl * 2 + 1 - c, 2 - 2 * xl + c, 3 - 2 * xl - c]
-    place = jnp.stack([xh] + quarters + [c, 1 - c]).astype(jnp.int32)
-
-    lat = lat_corr.reshape(64, 16, 4, 16).transpose(0, 2, 1, 3).reshape(64, 2, 512)
-    lat = lax.dynamic_index_in_dim(lat, c, 1, keepdims=False)
-    lat0 = lax.all_gather(lat, lats, axis=0, tiled=True)
-    lat0 = after(lat0, paired)
-    lat1 = lax.ppermute(lat0, "c", swap)
-
-    dev = deviations.reshape(64, 4, 8, 256)
-    made = jax.ShapeDtypeStruct((2, 2, 256, 256), BF16)
-    done = call(smooth_kernel, made, 4, work=30_000_000)(mine, sibling, lon_corr, across)
+    made = jax.ShapeDtypeStruct((2, 1024, 256), F32)
+    begun = call(smooth_kernel, made, 5, smem=(0,), work=30_000_000)(
+        place, mine, sibling, lon_corr, across
+    )
     res = call(
         correlate_kernel,
         jax.ShapeDtypeStruct((32, 64, 256), BF16),
         8,
         smem=(0,),
         scratch=[pltpu.VMEM((2, 1024, 256), BF16)],
-        before=(past,),
-    )(place, lat0, lat1, done, paired, opposite, lon_corr, across)
-    res = lax.all_to_all(res, ("zh", "y", "xh"), 0, 0, tiled=True)
+        before=(wide,),
+    )(place, lat0, lat1, begun, paired, opposite, lon_corr, across)
+    groups = [[p * 4 + k for p in range(16) for k in pair] for pair in ((0, 3), (1, 2))]
+    res = lax.all_to_all(
+        res, ("zh", "y", "xh", "xl"), 0, 0, axis_index_groups=groups, tiled=True
+    )
+    turned = jnp.stack([jnp.bitwise_xor(xh, xl)]).astype(jnp.int32)
 
     out = pl.pallas_call(
         final_kernel,
         grid=(4,),
         out_shape=jax.ShapeDtypeStruct((64, 4, 8, 256), F32),
-        in_specs=[big, big, big, pl.BlockSpec((32, 16, 256), lambda i: (0, i, 0))],
+        in_specs=[pl.BlockSpec(memory_space=pltpu.SMEM), big, big, pl.BlockSpec((32, 16, 256), lambda i: (0, i, 0))],
         out_specs=big,
         scratch_shapes=[pltpu.VMEM((2, 128, 128), F32)],
         compiler_params=params,
         cost_estimate=free,
-    )(inc, past, dev, res)
+    )(turned, base, dev, res)
     return out.reshape(increments.shape)
 
 

time: 163 us -> 154 us (0.945)
  blocking collectives: 41.9 us -> 0 us
  waiting for transfers between devices: 37.9 us -> 63.4 us
  other arithmetic: 2.08 us -> 6.81 us
  Pallas kernels: 19 us -> 22.6 us
    all_to_all x1 -> x0, blocking collectives: 41.9 us -> none  [body(): res = lax.all_to_all(res, ('zh', 'y', 'xh'), 0, 0, tiled=True)]
    all_to_all x1 -> x2, waiting for transfers between devices: 0.01 us -> 16.8 us  [the longest x1 12.3 us: body(): lax.all_to_all(res, ('zh', 'y', 'xh', 'xl'), 0, 0, axis_index_groups=grou...]
    all_gather x1, waiting for transfers between devices: 5.76 us -> 21.4 us  [body(): lat0 = after(lax.all_gather(lat, lats, axis=0, tiled=True), paired)]
    ppermute x1, waiting for transfers between devices: 10.6 us -> 1.57 us  [body(): left = lax.ppermute(wide[..., 254:], ('xh', 'xl', 'c'), ring)]
    unnamed x28 -> x40, local copies, waits for them, and re-layouts: 6.36 us -> 9.87 us
    all_to_all x1 -> x2, starting transfers between devices: 15 us -> 18.4 us  [the longest x1 11.6 us: body(): mine = lax.all_to_all(parts, ('zh', 'y', 'xl'), 0, 0, tiled=True)]
    pallas_call x2, Pallas kernels: 7.85 us -> 10.7 us  [call(): return lambda *args: made(*args, *before)]
    ppermute x1, starting transfers between devices: 2.96 us -> 0.28 us  [body(): right = lax.ppermute(wide[..., :2], ('xh', 'xl', 'c'), back)]
  transfers between devices with their start and end apart: 12 -> 13, of which waited for: 7 -> 9; matrix products, arithmetic and copies ran while one was open for 8% -> 8% of each run, Pallas kernels for 5% -> 7%
where the time goes in v3:
time: 154 us; the launch traced here: 153 us
  waiting for transfers between devices  63.4 us (41%)
  starting transfers between devices  31.4 us (20%)
  Pallas kernels  22.6 us (15%)
  local copies, waits for them, and re-layouts  15.4 us (10%)
  between operations  13.6 us (9%)
  other arithmetic  6.81 us (4%)
    all_gather x1, waiting for transfers between devices, body(): lat0 = after(lax.all_gather(lat, lats, axis=0, tiled=True), paired)  21.4 us
    all_to_all x1, waiting for transfers between devices, body(): lax.all_to_all(res, ('zh', 'y', 'xh', 'xl'), 0, 0, axis_index_groups=grou...  12.3 us
    all_to_all x1, starting transfers between devices, body(): mine = lax.all_to_all(parts, ('zh', 'y', 'xl'), 0, 0, tiled=True)  11.6 us
    pallas_call x2, Pallas kernels, call(): return lambda *args: made(*args, *before)  10.7 us
    ppermute x1, waiting for transfers between devices, body(): lax.ppermute(lon_corr, ('xh', 'xl'), [(i, 3 - i) for i in range(4)])  10.4 us
    unnamed x40, local copies, waits for them, and re-layouts  9.87 us
    ppermute x1, waiting for transfers between devices, body(): wide = lax.ppermute(wide, 'tm', [(0, 1)])  7.18 us
    all_to_all x1, starting transfers between devices, body(): lax.all_to_all(res, ('zh', 'y', 'xh', 'xl'), 0, 0, axis_index_groups=grou...  6.71 us
  transfers between devices with their start and end apart: 13, of which 9 were waited for; matrix products, arithmetic and copies ran while one was open for 8% of the time, Pallas kernels for 7%

profile of v3, /device:TPU:32, one launch (start us, length us, event | category | flops | bytes accessed | tf_op | source)
XLA Modules:
  0.0 153.1 jit_solution(10149445159364349150)
XLA Ops:
  6.5 0.0 copy-start
  6.5 0.9 copy-done
  7.5 1.2 copy-done.14
  8.7 1.9 %shard_map.74 = bf16[32,64,256]{2,1,0:T(8,128)(2,1)} custom-call(bf16[64,4,8,256]{3,2,1,0:T(8,128)(2,1)S(1)} %bitcast.29, bf16[64,512]{1,0:T(8,128)(2,1)S(1)} %constant_dynamic-slice_fusion.lat), custom_call_target="tpu_custom_call" | custom-call | tf_op jit(solution)/shard_map/pallas_call | solution.py:154
  10.6 0.0 copy-done.15
  10.7 11.6 %all-to-all-start = ((bf16[32,64,256]{2,1,0:T(8,128)(2,1)}), bf16[32,64,256]{2,1,0:T(8,128)(2,1)S(1)}, u32[]{:S(2)}, u32[]{:S(2)}) async-start(bf16[32,64,256]{2,1,0:T(8,128)(2,1)} %shard_map.74), calls=%async_computation | async-start | bytes 2097152 | tf_op jit(solution)/shard_map/all_to_all | solution.py:169
  22.3 0.0 all-gather.2.cloned.1.call-start
  22.4 0.0 copy-done.10
  22.4 3.1 %collective-permute-start.5 = (bf16[256,2048]{1,0:T(8,128)(2,1)S(1)}, bf16[256,2048]{1,0:T(8,128)(2,1)S(1)}, u32[]{:S(2)}, u32[]{:S(2)}) collective-permute-start(bf16[256,2048]{1,0:T(8,128)(2,1)S(1)} %copy-done.10), channel_id=1, source_target_pairs={{0,6},{2,4},{4,2},{6,0},{1,7},{3,5},{5,3},{7,1},{8,14},{10,12},{12... | collective-permute-start | bytes 3145736 | tf_op jit(solution)/shard_map/ppermute | solution.py:151
  25.5 0.0 all-gather.2.cloned.1.call-update
  25.5 2.8 %bitcast_convert_fusion.1 = (bf16[64,4,8,256]{3,2,1,0:T(8,128)(2,1)}, bf16[64,1,4,8,256]{4,3,2,0,1:T(8,128)(2,1)S(1)}) fusion(f32[64,1,4,8,256]{4,3,2,1,0:T(8,128)} %param.9), kind=kLoop, calls=%fused_computation.8 | loop fusion | flops 1048576 | bytes 4194304 | tf_op jit(solution)/shard_map/convert_element_type | solution.py:181
  28.3 3.4 %collective-permute-start = (bf16[2,4,8,256]{3,2,1,0:T(8,128)(2,1)S(1)}, bf16[2,4,8,256]{3,2,1,0:T(8,128)(2,1)S(1)}, u32[]{:S(2)}, u32[]{:S(2)}) collective-permute-start(bf16[2,4,8,256]{3,2,1,0:T(8,128)(2,1)S(1)} %get-tuple-element.9), channel_id=1, source_target_pairs={{0,8},{8,16},{16,24},{24,32},{32,40},{40,48},{48,56},{56,64},{64,7... | collective-permute-start | bytes 98312 | tf_op jit(solution)/shard_map/ppermute | solution.py:167
  31.7 1.3 collective-permute-start.1
  33.0 0.4 collective-permute-done.refs_2_
  33.4 4.5 %collective-permute-done.1.refs_3_ = bf16[2,4,8,256]{3,2,1,0:T(8,128)(2,1)S(1)} collective-permute-done((bf16[2,4,8,256]{3,2,1,0:T(8,128)(2,1)S(1)}, bf16[2,4,8,256]{3,2,1,0:T(8,128)(2,1)S(1)}, u32[]{:S(2)}, u32[]{:S(2)}) %collective-permute-start.1) | collective-permute-done | bytes 32800 | tf_op jit(solution)/shard_map/ppermute | solution.py:168
  37.9 10.4 %collective-permute-done.5.refs_1_.refs_4_.refs_7_ = bf16[256,2048]{1,0:T(8,128)(2,1)S(1)} collective-permute-done((bf16[256,2048]{1,0:T(8,128)(2,1)S(1)}, bf16[256,2048]{1,0:T(8,128)(2,1)S(1)}, u32[]{:S(2)}, u32[]{:S(2)}) %collective-permute-start.5) | collective-permute-done | bytes 1048608 | tf_op jit(solution)/shard_map/ppermute | solution.py:151
  48.3 4.5 %all-to-all-done = bf16[32,64,256]{2,1,0:T(8,128)(2,1)S(1)} async-done(((bf16[32,64,256]{2,1,0:T(8,128)(2,1)}), bf16[32,64,256]{2,1,0:T(8,128)(2,1)S(1)}, u32[]{:S(2)}, u32[]{:S(2)}) %all-to-all-start) | async-done | bytes 1048608 | tf_op jit(solution)/shard_map/all_to_all | solution.py:169
  52.8 0.0 copy-done.16
  52.8 0.0 copy-done.17
  52.8 0.0 copy-done.5
  52.8 1.0 copy-done.3
  53.8 2.7 %collective-permute-start.6 = (bf16[16,2,64,256]{3,2,1,0:T(8,128)(2,1)}, bf16[16,2,64,256]{3,2,1,0:T(8,128)(2,1)}, u32[]{:S(2)}, u32[]{:S(2)}) collective-permute-start(bf16[16,2,64,256]{3,2,1,0:T(8,128)(2,1)} %shard_map.75.refs_1_), channel_id=1, source_target_pairs={{0,4},{4,0},{1,5},{5,1},{2,6},{6,2},{3,7},{7,3},{8,12},{12,8},{9,1... | collective-permute-start | bytes 3145736 | tf_op jit(solution)/shard_map/ppermute | solution.py:171
  56.5 2.5 %pad_maximum_fusion = bf16[68,4,8,256]{3,2,1,0:T(8,128)(2,1)} fusion(bf16[2,4,8,256]{3,2,1,0:T(8,128)(2,1)} %copy-done.17, bf16[64,4,8,256]{3,2,1,0:T(8,128)(2,1)} %get-tuple-element.5, bf16[2,4,8,256]{3,2,1,0:T(8,128)(2,1)} %copy-done.16), kind=kLoop, calls=%fused_computation.1 | loop fusion | flops 1114112 | bytes 2228224 | tf_op jit(solution)/shard_map/concatenate | solution.py:181
  59.0 1.4 collective-permute-start.2
  60.4 0.0 copy-done.4
  60.4 0.1 collective-permute-start.8
  60.5 21.4 %all-gather.2.cloned.1.call-done.refs_0_ = bf16[1024,512]{1,0:T(8,128)(2,1)} async-done(((bf16[64,512]{1,0:T(8,128)(2,1)}), bf16[1024,512]{1,0:T(8,128)(2,1)}) %all-gather.2.cloned.1.call-update) | async-done | bytes 1048592 | tf_op jit(solution)/shard_map/all_gather | solution.py:177
  82.0 0.0 collective-permute-done.6.refs_1_.refs_4_
  82.0 0.0 collective-permute-start.7
  82.0 0.5 collective-permute-start.9
  82.5 0.1 stack.35.refs_0_
  82.6 0.0 collective-permute-done.8.refs_2_
  82.6 0.0 copy-start.11
  82.6 1.2 copy-done.11
  83.8 4.0 %shard_map.77.refs_3_ = f32[2,1024,256]{2,1,0:T(8,128)} custom-call(s32[7]{0:T(128)S(1)} %stack.35.refs_0_, bf16[16,2,64,256]{3,2,1,0:T(8,128)(2,1)S(1)} %copy-done.4, bf16[16,2,64,256]{3,2,1,0:T(8,128)(2,1)} %collective-permute-done.8.refs_2_, bf16[256,2048]{1,0:T(8,128)(2,1)S(1)} %copy-done.11, bf16[256,2048]{1,0:T(8,128)(2,1)S(1)} %copy-done.6), custom_call_target="tpu_custom_call" | custom-call | bytes 30000000 | tf_op jit(solution)/shard_map/pallas_call | solution.py:31
  87.8 7.2 %collective-permute-done.2.field.refs_8_ = bf16[68,4,8,256]{3,2,1,0:T(8,128)(2,1)S(1)} collective-permute-done((bf16[68,4,8,256]{3,2,1,0:T(8,128)(2,1)}, bf16[68,4,8,256]{3,2,1,0:T(8,128)(2,1)S(1)}, u32[]{:S(2)}, u32[]{:S(2)}) %collective-permute-start.2) | collective-permute-done | bytes 1114144 | tf_op jit(solution)/shard_map/ppermute | solution.py:182
  95.0 0.0 collective-permute-done.7.refs_2_
  95.0 0.0 collective-permute-done.9.refs_5_
  95.0 1.0 copy-done.1
  96.0 6.7 %shard_map.78 = bf16[32,64,256]{2,1,0:T(8,128)(2,1)} custom-call(s32[7]{0:T(128)S(1)} %stack.35.refs_0_, bf16[1024,512]{1,0:T(8,128)(2,1)S(1)} %copy-done.12, bf16[1024,512]{1,0:T(8,128)(2,1)} %collective-permute-done.7.refs_2_, f32[2,1024,256]{2,1,0:T(8,128)} %shard_map.77.refs_3_, bf16[16,2,64,256]{3,2,1,0:T(8,128)(2,1)} %collective-permute-done.6.refs_1_.refs_4_, ...), custom_call_target="tpu_custom_call" | custom-call | tf_op jit(solution)/shard_map/pallas_call | solution.py:31
  102.7 6.7 %all-to-all-start.1 = ((bf16[32,64,256]{2,1,0:T(8,128)(2,1)}), bf16[32,64,256]{2,1,0:T(8,128)(2,1)}, u32[]{:S(2)}, u32[]{:S(2)}) async-start(bf16[32,64,256]{2,1,0:T(8,128)(2,1)} %shard_map.78), calls=%async_computation.1 | async-start | bytes 2097152 | tf_op jit(solution)/shard_map/all_to_all | solution.py:214
  109.4 0.3 fusion
  109.7 0.0 copy-start.18
  109.7 0.7 copy.13
  110.4 0.3 collective-permute-start.3
  110.7 0.7 copy.14
  111.4 0.2 collective-permute-start.4
  111.6 0.0 copy-done.18
  111.6 0.1 pad.1.clone
  111.7 1.0 collective-permute-done.3
  112.7 1.7 %copy.15 = bf16[68,4,8,2]{3,2,1,0:T(8,128)(2,1)} copy(bf16[68,4,8,2]{0,2,3,1:T(8,128)(2,1)S(1)} %collective-permute-done.3) | data formatting | bytes 17408 | tf_op jit(solution)/shard_map/ppermute | solution.py:186
  114.4 1.6 %collective-permute-done.4 = bf16[68,4,8,2]{0,2,3,1:T(8,128)(2,1)S(1)} collective-permute-done((bf16[68,4,8,2]{0,2,3,1:T(8,128)(2,1)S(1)}, bf16[68,4,8,2]{0,2,3,1:T(8,128)(2,1)S(1)}, u32[]{:S(2)}, u32[]{:S(2)}) %collective-permute-start.4) | collective-permute-done | bytes 8736 | tf_op jit(solution)/shard_map/ppermute | solution.py:185
  116.0 1.7 %copy.16 = bf16[68,4,8,2]{3,2,1,0:T(8,128)(2,1)} copy(bf16[68,4,8,2]{0,2,3,1:T(8,128)(2,1)S(1)} %collective-permute-done.4) | data formatting | bytes 17408 | tf_op jit(solution)/shard_map/ppermute | solution.py:185
  117.7 1.6 %pad_maximum_fusion.1.rim = bf16[68,4,8,128]{3,2,1,0:T(8,128)(2,1)S(1)} fusion(bf16[68,4,8,2]{3,2,1,0:T(8,128)(2,1)} %copy.16, bf16[68,4,8,2]{3,2,1,0:T(8,128)(2,1)} %copy.15, bf16[128]{0:T(256)(128)(2,1)S(1)} %pad.1.clone), kind=kLoop, calls=%fused_computation.2 | loop fusion | flops 1671168 | bytes 574720 | tf_op jit(solution)/shard_map/concatenate | solution.py:187
  119.3 0.1 broadcast_in_dim.23.off0
  119.3 0.1 broadcast_in_dim.25.off1
  119.4 0.1 broadcast_in_dim.26.courant
  119.5 6.0 %shard_map.73.base = f32[64,4,8,256]{3,2,1,0:T(8,128)S(1)} custom-call(f32[64,4,8,256]{3,2,1,0:T(8,128)S(1)} %bitcast.27, bf16[68,4,8,256]{3,2,1,0:T(8,128)(2,1)S(1)} %copy-done.2, bf16[68,4,8,128]{3,2,1,0:T(8,128)(2,1)S(1)} %pad_maximum_fusion.1.rim, s32[8,384]{1,0:T(8,128)S(1)} %broadcast_in_dim.23.off0, s32[8,384]{1,0:T(8,128)S(1)} %broadcast_in_dim.25.off1, ...), custom_call_target="tpu_custom_call" | custom-call | bytes 20000000 | tf_op jit(solution)/shard_map/pallas_call | solution.py:190
  125.5 0.0 copy-start.8
  125.5 1.3 copy-done.8
  126.8 12.3 %all-to-all-done.1.got = bf16[32,64,256]{2,1,0:T(8,128)(2,1)} async-done(((bf16[32,64,256]{2,1,0:T(8,128)(2,1)}), bf16[32,64,256]{2,1,0:T(8,128)(2,1)}, u32[]{:S(2)}, u32[]{:S(2)}) %all-to-all-start.1) | async-done | bytes 1048608 | tf_op jit(solution)/shard_map/all_to_all | solution.py:214
  139.2 1.6 %copy-done.9 = f32[64,4,8,256]{3,2,1,0:T(8,128)S(1)} copy-done((f32[64,4,8,256]{3,2,1,0:T(8,128)S(1)}, f32[64,4,8,256]{3,2,1,0:T(8,128)}, u32[]{:S(2)}) %copy-start.9) | copy-done | bytes 2097176
  140.7 1.6 %copy-done.13 = f32[64,1,4,8,256]{4,3,2,1,0:T(8,128)S(1)} copy-done((f32[64,1,4,8,256]{4,3,2,1,0:T(8,128)S(1)}, f32[64,1,4,8,256]{4,3,2,1,0:T(8,128)}, u32[]{:S(2)}) %copy-start.13) | copy-done | bytes 2097176
  142.3 3.9 %shard_map.79 = f32[64,4,8,256]{3,2,1,0:T(8,128)} custom-call(s32[1]{0:T(128)} %bitcast.turned, f32[64,4,8,256]{3,2,1,0:T(8,128)S(1)} %copy-done.9, f32[64,4,8,256]{3,2,1,0:T(8,128)S(1)} %bitcast.28, bf16[32,64,256]{2,1,0:T(8,128)(2,1)} %all-to-all-done.1.got), custom_call_target="tpu_custom_call" | custom-call | tf_op jit(solution)/shard_map/pallas_call | solution.py:219
  (27 shorter events, 0.1 us)
Async XLA Ops:
  6.5 0.9 copy-start
  7.4 3.2 %copy-start.15 = (bf16[64,512]{1,0:T(8,128)(2,1)}, bf16[64,512]{1,0:T(8,128)(2,1)S(1)}, u32[]{:S(2)}) copy-start(bf16[64,512]{1,0:T(8,128)(2,1)S(1)} %constant_dynamic-slice_fusion.lat) | copy-start | bytes 196612
  7.4 1.2 copy-start.14
  10.6 11.7 %copy-start.10 = (bf16[256,2048]{1,0:T(8,128)(2,1)S(1)}, bf16[256,2048]{1,0:T(8,128)(2,1)}, u32[]{:S(2)}) copy-start(bf16[256,2048]{1,0:T(8,128)(2,1)} %refs_6_.1) | copy-start | bytes 3145732
  10.7 42.2 %all-to-all-start = ((bf16[32,64,256]{2,1,0:T(8,128)(2,1)}), bf16[32,64,256]{2,1,0:T(8,128)(2,1)S(1)}, u32[]{:S(2)}, u32[]{:S(2)}) async-start(bf16[32,64,256]{2,1,0:T(8,128)(2,1)} %shard_map.74), calls=%async_computation | async-start | bytes 2097152 | tf_op jit(solution)/shard_map/all_to_all | solution.py:169
  22.3 59.7 %all-gather.2.cloned.1.call-start = ((), (), s32[]{:S(2)}) async-start(), calls=%async_computation.2 | async-start | bytes 1114112 | tf_op jit(solution)/shard_map/all_gather | solution.py:177
  22.4 25.9 %collective-permute-start.5 = (bf16[256,2048]{1,0:T(8,128)(2,1)S(1)}, bf16[256,2048]{1,0:T(8,128)(2,1)S(1)}, u32[]{:S(2)}, u32[]{:S(2)}) collective-permute-start(bf16[256,2048]{1,0:T(8,128)(2,1)S(1)} %copy-done.10), channel_id=1, source_target_pairs={{0,6},{2,4},{4,2},{6,0},{1,7},{3,5},{5,3},{7,1},{8,14},{10,12},{12... | collective-permute-start | bytes 3145736 | tf_op jit(solution)/shard_map/ppermute | solution.py:151
  28.3 5.1 %collective-permute-start = (bf16[2,4,8,256]{3,2,1,0:T(8,128)(2,1)S(1)}, bf16[2,4,8,256]{3,2,1,0:T(8,128)(2,1)S(1)}, u32[]{:S(2)}, u32[]{:S(2)}) collective-permute-start(bf16[2,4,8,256]{3,2,1,0:T(8,128)(2,1)S(1)} %get-tuple-element.9), channel_id=1, source_target_pairs={{0,8},{8,16},{16,24},{24,32},{32,40},{40,48},{48,56},{56,64},{64,7... | collective-permute-start | bytes 98312 | tf_op jit(solution)/shard_map/ppermute | solution.py:167
  31.7 6.2 %collective-permute-start.1 = (bf16[2,4,8,256]{3,2,1,0:T(8,128)(2,1)S(1)}, bf16[2,4,8,256]{3,2,1,0:T(8,128)(2,1)S(1)}, u32[]{:S(2)}, u32[]{:S(2)}) collective-permute-start(bf16[2,4,8,256]{3,2,1,0:T(8,128)(2,1)S(1)} %get-tuple-element.10), channel_id=1, source_target_pairs={{8,0},{16,8},{24,16},{32,24},{40,32},{48,40},{56,48},{64,56},{72,6... | collective-permute-start | bytes 98312 | tf_op jit(solution)/shard_map/ppermute | solution.py:168
  33.4 19.5 %copy-start.16 = (bf16[2,4,8,256]{3,2,1,0:T(8,128)(2,1)}, bf16[2,4,8,256]{3,2,1,0:T(8,128)(2,1)S(1)}, u32[]{:S(2)}) copy-start(bf16[2,4,8,256]{3,2,1,0:T(8,128)(2,1)S(1)} %collective-permute-done.refs_2_) | copy-start | bytes 98308
  37.9 14.9 %copy-start.17 = (bf16[2,4,8,256]{3,2,1,0:T(8,128)(2,1)}, bf16[2,4,8,256]{3,2,1,0:T(8,128)(2,1)S(1)}, u32[]{:S(2)}) copy-start(bf16[2,4,8,256]{3,2,1,0:T(8,128)(2,1)S(1)} %collective-permute-done.1.refs_3_) | copy-start | bytes 98308
  48.3 4.5 %copy-start.5 = (bf16[256,2048]{1,0:T(8,128)(2,1)}, bf16[256,2048]{1,0:T(8,128)(2,1)S(1)}, u32[]{:S(2)}) copy-start(bf16[256,2048]{1,0:T(8,128)(2,1)S(1)} %collective-permute-done.5.refs_1_.refs_4_.refs_7_) | copy-start | bytes 3145732
  52.8 1.0 copy-start.3
  53.8 28.2 %collective-permute-start.6 = (bf16[16,2,64,256]{3,2,1,0:T(8,128)(2,1)}, bf16[16,2,64,256]{3,2,1,0:T(8,128)(2,1)}, u32[]{:S(2)}, u32[]{:S(2)}) collective-permute-start(bf16[16,2,64,256]{3,2,1,0:T(8,128)(2,1)} %shard_map.75.refs_1_), channel_id=1, source_target_pairs={{0,4},{4,0},{1,5},{5,1},{2,6},{6,2},{3,7},{7,3},{8,12},{12,8},{9,1... | collective-permute-start | bytes 3145736 | tf_op jit(solution)/shard_map/ppermute | solution.py:171
  56.5 3.9 %copy-start.4 = (bf16[16,2,64,256]{3,2,1,0:T(8,128)(2,1)S(1)}, bf16[16,2,64,256]{3,2,1,0:T(8,128)(2,1)}, u32[]{:S(2)}) copy-start(bf16[16,2,64,256]{3,2,1,0:T(8,128)(2,1)} %shard_map.75.refs_1_) | copy-start | bytes 3145732
  59.0 23.6 %copy-start.6 = (bf16[256,2048]{1,0:T(8,128)(2,1)S(1)}, bf16[256,2048]{1,0:T(8,128)(2,1)}, u32[]{:S(2)}) copy-start(bf16[256,2048]{1,0:T(8,128)(2,1)} %copy-done.5) | copy-start | bytes 3145732
  59.0 35.9 %collective-permute-start.2 = (bf16[68,4,8,256]{3,2,1,0:T(8,128)(2,1)}, bf16[68,4,8,256]{3,2,1,0:T(8,128)(2,1)S(1)}, u32[]{:S(2)}, u32[]{:S(2)}) collective-permute-start(bf16[68,4,8,256]{3,2,1,0:T(8,128)(2,1)} %pad_maximum_fusion), channel_id=1, source_target_pairs={{0,128},{1,129},{2,130},{3,131},{4,132},{5,133},{6,134},{7,135},{8... | collective-permute-start | bytes 3342344 | tf_op jit(solution)/shard_map/ppermute | solution.py:182
  60.4 22.1 %collective-permute-start.8 = (bf16[16,2,64,256]{3,2,1,0:T(8,128)(2,1)S(1)}, bf16[16,2,64,256]{3,2,1,0:T(8,128)(2,1)}, u32[]{:S(2)}, u32[]{:S(2)}) collective-permute-start(bf16[16,2,64,256]{3,2,1,0:T(8,128)(2,1)S(1)} %copy-done.4), channel_id=1, source_target_pairs={{0,1},{1,0},{2,3},{3,2},{4,5},{5,4},{6,7},{7,6},{8,9},{9,8},{10,11... | collective-permute-start | bytes 3145736 | tf_op jit(solution)/shard_map/ppermute | solution.py:172
  82.0 13.0 %collective-permute-start.7 = (bf16[1024,512]{1,0:T(8,128)(2,1)}, bf16[1024,512]{1,0:T(8,128)(2,1)}, u32[]{:S(2)}, u32[]{:S(2)}) collective-permute-start(bf16[1024,512]{1,0:T(8,128)(2,1)} %shard_map.76.refs_1_), channel_id=1, source_target_pairs={{0,1},{1,0},{2,3},{3,2},{4,5},{5,4},{6,7},{7,6},{8,9},{9,8},{10,11... | collective-permute-start | bytes 3145736 | tf_op jit(solution)/shard_map/ppermute | solution.py:178
  82.0 13.0 %collective-permute-start.9 = (bf16[16,2,64,256]{3,2,1,0:T(8,128)(2,1)}, bf16[16,2,64,256]{3,2,1,0:T(8,128)(2,1)}, u32[]{:S(2)}, u32[]{:S(2)}) collective-permute-start(bf16[16,2,64,256]{3,2,1,0:T(8,128)(2,1)} %collective-permute-done.6.refs_1_.refs_4_), channel_id=1, source_target_pairs={{0,1},{1,0},{2,3},{3,2},{4,5},{5,4},{6,7},{7,6},{8,9},{9,8},{10,11... | collective-permute-start | bytes 3145736 | tf_op jit(solution)/shard_map/ppermute | solution.py:173
  82.6 1.2 copy-start.11
  83.8 12.2 %copy-start.12 = (bf16[1024,512]{1,0:T(8,128)(2,1)S(1)}, bf16[1024,512]{1,0:T(8,128)(2,1)}, u32[]{:S(2)}) copy-start(bf16[1024,512]{1,0:T(8,128)(2,1)} %shard_map.76.refs_1_) | copy-start | bytes 3145732
  95.0 1.0 copy-start.1
  102.7 6.7 %copy-start.2 = (bf16[68,4,8,256]{3,2,1,0:T(8,128)(2,1)S(1)}, bf16[68,4,8,256]{3,2,1,0:T(8,128)(2,1)}, u32[]{:S(2)}) copy-start(bf16[68,4,8,256]{3,2,1,0:T(8,128)(2,1)} %copy-done.1) | copy-start | bytes 3342340
  102.7 36.5 %all-to-all-start.1 = ((bf16[32,64,256]{2,1,0:T(8,128)(2,1)}), bf16[32,64,256]{2,1,0:T(8,128)(2,1)}, u32[]{:S(2)}, u32[]{:S(2)}) async-start(bf16[32,64,256]{2,1,0:T(8,128)(2,1)} %shard_map.78), calls=%async_computation.1 | async-start | bytes 2097152 | tf_op jit(solution)/shard_map/all_to_all | solution.py:214
  109.7 1.9 %copy-start.18 = (s32[2,8]{1,0:T(2,128)S(1)}, s32[2,8]{1,0:T(2,128)}, u32[]{:S(2)}) copy-start(s32[2,8]{1,0:T(2,128)} %param.12) | copy-start | bytes 196
  110.4 2.3 %collective-permute-start.3 = (bf16[68,4,8,2]{0,2,3,1:T(8,128)(2,1)S(1)}, bf16[68,4,8,2]{0,2,3,1:T(8,128)(2,1)S(1)}, u32[]{:S(2)}, u32[]{:S(2)}) collective-permute-start(bf16[68,4,8,2]{0,2,3,1:T(8,128)(2,1)S(1)} %copy.13), channel_id=1, source_target_pairs={{1,0},{2,1},{3,2},{4,3},{5,4},{6,5},{7,6},{0,7},{9,8},{10,9},{11,1... | collective-permute-start | bytes 26120 | tf_op jit(solution)/shard_map/ppermute | solution.py:186
  111.4 4.6 %collective-permute-start.4 = (bf16[68,4,8,2]{0,2,3,1:T(8,128)(2,1)S(1)}, bf16[68,4,8,2]{0,2,3,1:T(8,128)(2,1)S(1)}, u32[]{:S(2)}, u32[]{:S(2)}) collective-permute-start(bf16[68,4,8,2]{0,2,3,1:T(8,128)(2,1)S(1)} %copy.14), channel_id=1, source_target_pairs={{0,1},{1,2},{2,3},{3,4},{4,5},{5,6},{6,7},{7,0},{8,9},{9,10},{10,1... | collective-permute-start | bytes 26120 | tf_op jit(solution)/shard_map/ppermute | solution.py:185
  114.4 5.0 %copy-start.19 = (f32[4]{0:T(128)S(1)}, f32[4]{0:T(128)}, u32[]{:S(2)}) copy-start(f32[4]{0:T(128)} %param.13) | copy-start | bytes 52
  114.4 5.1 %copy-start.7 = (f32[64,1,4,8,256]{4,3,2,1,0:T(8,128)S(1)}, f32[64,1,4,8,256]{4,3,2,1,0:T(8,128)}, u32[]{:S(2)}) copy-start(f32[64,1,4,8,256]{4,3,2,1,0:T(8,128)} %param.9) | copy-start | bytes 6291460
  125.5 1.3 copy-start.8
  139.2 1.6 %copy-start.9 = (f32[64,4,8,256]{3,2,1,0:T(8,128)S(1)}, f32[64,4,8,256]{3,2,1,0:T(8,128)}, u32[]{:S(2)}) copy-start(f32[64,4,8,256]{3,2,1,0:T(8,128)} %copy-done.8) | copy-start | bytes 6291460
  140.7 1.6 %copy-start.13 = (f32[64,1,4,8,256]{4,3,2,1,0:T(8,128)S(1)}, f32[64,1,4,8,256]{4,3,2,1,0:T(8,128)}, u32[]{:S(2)}) copy-start(f32[64,1,4,8,256]{4,3,2,1,0:T(8,128)} %param.8) | copy-start | bytes 6291460
Sparse Core Ops, SparseCore 0:
  25.7 56.2 all-gather.1

commit v4 on v3

--- a/solution.py
+++ b/solution.py
@@ -167,18 +167,24 @@
     low = lax.ppermute(inc[62:].astype(BF16), lats, [(i, i + 1) for i in range(15)])
     high = lax.ppermute(inc[:2].astype(BF16), lats, [(i + 1, i) for i in range(15)])
     mine = lax.all_to_all(parts, ("zh", "y", "xl"), 0, 0, tiled=True)
-    mine = after(mine.reshape(16, 2, 64, 256), across, low, high)
+    wide = jnp.concatenate([low, inc.astype(BF16), high], axis=0)
+    mine = after(mine.reshape(16, 2, 64, 256), across, wide)
     paired = lax.ppermute(mine, "xh", swap)
     sibling = lax.ppermute(mine, "c", swap)
-    opposite = lax.ppermute(paired, "c", swap)
     starts = [(a * 4 + b) * 256 for a in (xh, 1 - xh) for b in (c, 1 - c)]
     place = jnp.stack([xh] + starts + [c, 1 - c]).astype(jnp.int32)
 
+    made = jax.ShapeDtypeStruct((2, 1024, 256), F32)
+    begun = call(smooth_kernel, made, 5, smem=(0,), work=30_000_000)(
+        place, mine, sibling, lon_corr, across
+    )
+    paired = after(paired, begun)
+    opposite = lax.ppermute(paired, "c", swap)
+
     lat0 = after(lax.all_gather(lat, lats, axis=0, tiled=True), paired)
     lat1 = lax.ppermute(lat0, "c", swap)
 
     dev = deviations.reshape(64, 4, 8, 256)
-    wide = jnp.concatenate([low, inc.astype(BF16), high], axis=0)
     wide = lax.ppermute(wide, "tm", [(0, 1)])
     ring = [(i, (i + 1) % 8) for i in range(8)]
     back = [((i + 1) % 8, i) for i in range(8)]
@@ -198,10 +204,6 @@
         cost_estimate=pl.CostEstimate(flops=0, bytes_accessed=20_000_000, transcendentals=0),
     )(inc, wide, rim, off[0], off[1], jnp.broadcast_to(courant[:, None, None], (4, 8, 256)))
 
-    made = jax.ShapeDtypeStruct((2, 1024, 256), F32)
-    begun = call(smooth_kernel, made, 5, smem=(0,), work=30_000_000)(
-        place, mine, sibling, lon_corr, across
-    )
     res = call(
         correlate_kernel,
         jax.ShapeDtypeStruct((32, 64, 256), BF16),
@@ -223,7 +225,7 @@
         in_specs=[pl.BlockSpec(memory_space=pltpu.SMEM), big, big, pl.BlockSpec((32, 16, 256), lambda i: (0, i, 0))],
         out_specs=big,
         scratch_shapes=[pltpu.VMEM((2, 128, 128), F32)],
-        compiler_params=params,
+        compiler_params=pltpu.CompilerParams(vmem_limit_bytes=62 * 1024 * 1024),
         cost_estimate=free,
     )(turned, base, dev, res)
     return out.reshape(increments.shape)

time: 154 us -> 151 us (0.981)
  waiting for transfers between devices: 63.4 us -> 60.8 us
  other arithmetic: 6.81 us -> 4.59 us
    all_gather x1, waiting for transfers between devices: 21.4 us -> 0.01 us  [body(): lat0 = after(lax.all_gather(lat, lats, axis=0, tiled=True), paired)]
    ppermute x1, waiting for transfers between devices: 0.01 us -> 16.8 us  [body(): paired = lax.ppermute(mine, 'xh', swap)]
    ppermute x1, waiting for transfers between devices: 7.18 us -> 10.4 us  [body(): wide = lax.ppermute(wide, 'tm', [(0, 1)])]
    unnamed x40 -> x34, local copies, waits for them, and re-layouts: 9.87 us -> 11.4 us
  transfers between devices with their start and end apart: 13 -> 13, of which waited for: 9 -> 9; matrix products, arithmetic and copies ran while one was open for 8% -> 7% of each run, Pallas kernels for 7% -> 7%
where the time goes in v4:
time: 151 us
  waiting for transfers between devices  60.8 us (40%)
  starting transfers between devices  32.4 us (21%)
  Pallas kernels  22.2 us (15%)
  local copies, waits for them, and re-layouts  16.9 us (11%)
  between operations  13.6 us (9%)
  other arithmetic  4.59 us (3%)
    ppermute x1, waiting for transfers between devices, body(): paired = lax.ppermute(mine, 'xh', swap)  16.8 us
    all_to_all x1, starting transfers between devices, body(): mine = lax.all_to_all(parts, ('zh', 'y', 'xl'), 0, 0, tiled=True)  11.6 us
    all_to_all x1, waiting for transfers between devices, body(): lax.all_to_all(res, ('zh', 'y', 'xh', 'xl'), 0, 0, axis_index_groups=grou...  11.5 us
    unnamed x34, local copies, waits for them, and re-layouts  11.4 us
    ppermute x1, waiting for transfers between devices, body(): wide = lax.ppermute(wide, 'tm', [(0, 1)])  10.4 us
    ppermute x1, waiting for transfers between devices, body(): lax.ppermute(lon_corr, ('xh', 'xl'), [(i, 3 - i) for i in range(4)])  10.4 us
    pallas_call x2, Pallas kernels, call(): return lambda *args: made(*args, *before)  9.65 us
    all_to_all x1, starting transfers between devices, body(): lax.all_to_all(res, ('zh', 'y', 'xh', 'xl'), 0, 0, axis_index_groups=grou...  7.48 us
  transfers between devices with their start and end apart: 13, of which 9 were waited for; matrix products, arithmetic and copies ran while one was open for 7% of the time, Pallas kernels for 7%

profile of v4, /device:TPU:32, one launch (start us, length us, event | category | flops | bytes accessed | tf_op | source)
XLA Modules:
  0.0 150.5 jit_solution(14149332376116297046)
XLA Ops:
  6.5 0.0 copy-start
  6.5 0.9 copy-done
  7.5 1.2 copy-done.13
  8.7 1.9 %shard_map.74 = bf16[32,64,256]{2,1,0:T(8,128)(2,1)} custom-call(bf16[64,4,8,256]{3,2,1,0:T(8,128)(2,1)S(1)} %bitcast.28, bf16[64,512]{1,0:T(8,128)(2,1)S(1)} %constant_dynamic-slice_fusion.lat), custom_call_target="tpu_custom_call" | custom-call | tf_op jit(solution)/shard_map/pallas_call | solution.py:154
  10.6 0.0 copy-done.14
  10.6 11.6 %all-to-all-start = ((bf16[32,64,256]{2,1,0:T(8,128)(2,1)}), bf16[32,64,256]{2,1,0:T(8,128)(2,1)S(1)}, u32[]{:S(2)}, u32[]{:S(2)}) async-start(bf16[32,64,256]{2,1,0:T(8,128)(2,1)} %shard_map.74), calls=%async_computation | async-start | bytes 2097152 | tf_op jit(solution)/shard_map/all_to_all | solution.py:169
  22.3 0.0 all-gather.2.cloned.1.call-start
  22.3 0.0 copy-done.11
  22.4 3.1 %collective-permute-start.5 = (bf16[256,2048]{1,0:T(8,128)(2,1)S(1)}, bf16[256,2048]{1,0:T(8,128)(2,1)S(1)}, u32[]{:S(2)}, u32[]{:S(2)}) collective-permute-start(bf16[256,2048]{1,0:T(8,128)(2,1)S(1)} %copy-done.11), channel_id=1, source_target_pairs={{0,6},{2,4},{4,2},{6,0},{1,7},{3,5},{5,3},{7,1},{8,14},{10,12},{12... | collective-permute-start | bytes 3145736 | tf_op jit(solution)/shard_map/ppermute | solution.py:151
  25.5 0.0 all-gather.2.cloned.1.call-update
  25.5 1.9 %bitcast_convert_fusion.1 = (bf16[64,4,8,256]{3,2,1,0:T(8,128)(2,1)S(1)}, bf16[64,1,4,8,256]{4,3,2,0,1:T(8,128)(2,1)S(1)}) fusion(f32[64,1,4,8,256]{4,3,2,1,0:T(8,128)} %param.9), kind=kLoop, calls=%fused_computation.8 | loop fusion | flops 1048576 | bytes 4194304 | tf_op jit(solution)/shard_map/convert_element_type | solution.py:170
  27.4 3.4 %collective-permute-start = (bf16[2,4,8,256]{3,2,1,0:T(8,128)(2,1)S(1)}, bf16[2,4,8,256]{3,2,1,0:T(8,128)(2,1)S(1)}, u32[]{:S(2)}, u32[]{:S(2)}) collective-permute-start(bf16[2,4,8,256]{3,2,1,0:T(8,128)(2,1)S(1)} %get-tuple-element.9), channel_id=1, source_target_pairs={{0,8},{8,16},{16,24},{24,32},{32,40},{40,48},{48,56},{56,64},{64,7... | collective-permute-start | bytes 98312 | tf_op jit(solution)/shard_map/ppermute | solution.py:167
  30.8 1.3 collective-permute-start.1
  32.1 0.8 collective-permute-done
  32.9 3.9 %collective-permute-done.1 = bf16[2,4,8,256]{3,2,1,0:T(8,128)(2,1)S(1)} collective-permute-done((bf16[2,4,8,256]{3,2,1,0:T(8,128)(2,1)S(1)}, bf16[2,4,8,256]{3,2,1,0:T(8,128)(2,1)S(1)}, u32[]{:S(2)}, u32[]{:S(2)}) %collective-permute-start.1) | collective-permute-done | bytes 32800 | tf_op jit(solution)/shard_map/ppermute | solution.py:168
  36.7 1.2 pad_maximum_fusion.refs_2_
  37.9 10.4 %collective-permute-done.5.refs_1_.refs_4_.refs_7_ = bf16[256,2048]{1,0:T(8,128)(2,1)S(1)} collective-permute-done((bf16[256,2048]{1,0:T(8,128)(2,1)S(1)}, bf16[256,2048]{1,0:T(8,128)(2,1)S(1)}, u32[]{:S(2)}, u32[]{:S(2)}) %collective-permute-start.5) | collective-permute-done | bytes 1048608 | tf_op jit(solution)/shard_map/ppermute | solution.py:151
  48.3 4.5 %all-to-all-done = bf16[32,64,256]{2,1,0:T(8,128)(2,1)S(1)} async-done(((bf16[32,64,256]{2,1,0:T(8,128)(2,1)}), bf16[32,64,256]{2,1,0:T(8,128)(2,1)S(1)}, u32[]{:S(2)}, u32[]{:S(2)}) %all-to-all-start) | async-done | bytes 1048608 | tf_op jit(solution)/shard_map/all_to_all | solution.py:169
  52.8 0.0 copy-done.5
  52.8 1.0 copy-done.3
  53.8 0.0 collective-permute-start.7
  53.8 2.7 %collective-permute-start.6 = (bf16[16,2,64,256]{3,2,1,0:T(8,128)(2,1)}, bf16[16,2,64,256]{3,2,1,0:T(8,128)(2,1)S(1)}, u32[]{:S(2)}, u32[]{:S(2)}) collective-permute-start(bf16[16,2,64,256]{3,2,1,0:T(8,128)(2,1)} %shard_map.75.refs_1_), channel_id=1, source_target_pairs={{0,4},{4,0},{1,5},{5,1},{2,6},{6,2},{3,7},{7,3},{8,12},{12,8},{9,1... | collective-permute-start | bytes 3145736 | tf_op jit(solution)/shard_map/ppermute | solution.py:172
  56.6 1.3 collective-permute-start.2
  57.9 0.1 stack.35.refs_0_
  57.9 0.0 collective-permute-done.7.refs_2_
  57.9 1.2 copy-done.4
  59.2 1.2 copy-done.6
  60.4 3.9 %shard_map.76.refs_1_.refs_3_ = f32[2,1024,256]{2,1,0:T(8,128)} custom-call(s32[7]{0:T(128)S(1)} %stack.35.refs_0_, bf16[16,2,64,256]{3,2,1,0:T(8,128)(2,1)S(1)} %copy-done.4, bf16[16,2,64,256]{3,2,1,0:T(8,128)(2,1)} %collective-permute-done.7.refs_2_, bf16[256,2048]{1,0:T(8,128)(2,1)S(1)} %copy-done.11, bf16[256,2048]{1,0:T(8,128)(2,1)S(1)} %copy-done.6), custom_call_target="tpu_custom_call" | custom-call | bytes 30000000 | tf_op jit(solution)/shard_map/pallas_call | solution.py:31
  64.3 16.8 %collective-permute-done.6.refs_0_ = bf16[16,2,64,256]{3,2,1,0:T(8,128)(2,1)S(1)} collective-permute-done((bf16[16,2,64,256]{3,2,1,0:T(8,128)(2,1)}, bf16[16,2,64,256]{3,2,1,0:T(8,128)(2,1)S(1)}, u32[]{:S(2)}, u32[]{:S(2)}) %collective-permute-start.6) | collective-permute-done | bytes 1048608 | tf_op jit(solution)/shard_map/ppermute | solution.py:172
  81.1 1.0 copy-done.7
  82.1 0.0 collective-permute-start.8
  82.1 1.2 copy-done.8
  83.3 0.0 collective-permute-start.9
  83.3 10.4 %collective-permute-done.2.field.refs_8_ = bf16[68,4,8,256]{3,2,1,0:T(8,128)(2,1)S(1)} collective-permute-done((bf16[68,4,8,256]{3,2,1,0:T(8,128)(2,1)}, bf16[68,4,8,256]{3,2,1,0:T(8,128)(2,1)S(1)}, u32[]{:S(2)}, u32[]{:S(2)}) %collective-permute-start.2) | collective-permute-done | bytes 1114144 | tf_op jit(solution)/shard_map/ppermute | solution.py:188
  93.8 0.0 collective-permute-done.8.refs_2_
  93.8 0.0 collective-permute-done.9.refs_5_
  93.8 1.0 copy-done.1
  94.8 1.2 copy-done.12
  96.0 5.8 %shard_map.79 = bf16[32,64,256]{2,1,0:T(8,128)(2,1)} custom-call(s32[7]{0:T(128)S(1)} %stack.35.refs_0_, bf16[1024,512]{1,0:T(8,128)(2,1)S(1)} %copy-done.12, bf16[1024,512]{1,0:T(8,128)(2,1)S(1)} %collective-permute-done.8.refs_2_, f32[2,1024,256]{2,1,0:T(8,128)} %shard_map.76.refs_1_.refs_3_, bf16[16,2,64,256]{3,2,1,0:T(8,128)(2,1)S(1)} %copy-done.8, ...), custom_call_target="tpu_custom_call" | custom-call | tf_op jit(solution)/shard_map/pallas_call | solution.py:31
  101.8 7.5 %all-to-all-start.1 = ((bf16[32,64,256]{2,1,0:T(8,128)(2,1)}), bf16[32,64,256]{2,1,0:T(8,128)(2,1)}, u32[]{:S(2)}, u32[]{:S(2)}) async-start(bf16[32,64,256]{2,1,0:T(8,128)(2,1)} %shard_map.79), calls=%async_computation.1 | async-start | bytes 2097152 | tf_op jit(solution)/shard_map/all_to_all | solution.py:216
  109.3 0.0 copy-done.2
  109.3 0.3 fusion
  109.5 0.0 copy-start.15
  109.6 0.7 copy.14
  110.2 1.4 collective-permute-start.3
  111.6 0.7 copy.15
  112.3 0.0 collective-permute-start.4
  112.3 0.0 copy-done.15
  112.4 0.1 pad.1.clone
  112.4 0.6 collective-permute-done.3
  113.1 1.7 %copy.16 = bf16[68,4,8,2]{3,2,1,0:T(8,128)(2,1)} copy(bf16[68,4,8,2]{0,2,3,1:T(8,128)(2,1)S(1)} %collective-permute-done.3) | data formatting | bytes 17408 | tf_op jit(solution)/shard_map/ppermute | solution.py:192
  114.8 1.9 %collective-permute-done.4 = bf16[68,4,8,2]{0,2,3,1:T(8,128)(2,1)S(1)} collective-permute-done((bf16[68,4,8,2]{0,2,3,1:T(8,128)(2,1)S(1)}, bf16[68,4,8,2]{0,2,3,1:T(8,128)(2,1)S(1)}, u32[]{:S(2)}, u32[]{:S(2)}) %collective-permute-start.4) | collective-permute-done | bytes 8736 | tf_op jit(solution)/shard_map/ppermute | solution.py:191
  116.7 1.7 %copy.17 = bf16[68,4,8,2]{3,2,1,0:T(8,128)(2,1)} copy(bf16[68,4,8,2]{0,2,3,1:T(8,128)(2,1)S(1)} %collective-permute-done.4) | data formatting | bytes 17408 | tf_op jit(solution)/shard_map/ppermute | solution.py:191
  118.4 1.6 %pad_maximum_fusion.1.rim = bf16[68,4,8,128]{3,2,1,0:T(8,128)(2,1)S(1)} fusion(bf16[68,4,8,2]{3,2,1,0:T(8,128)(2,1)} %copy.17, bf16[68,4,8,2]{3,2,1,0:T(8,128)(2,1)} %copy.16, bf16[128]{0:T(256)(128)(2,1)S(1)} %pad.1.clone), kind=kLoop, calls=%fused_computation.2 | loop fusion | flops 1671168 | bytes 574720 | tf_op jit(solution)/shard_map/concatenate | solution.py:193
  120.0 0.1 broadcast_in_dim.23.off0
  120.1 0.1 broadcast_in_dim.25.off1
  120.1 0.0 copy-done.16
  120.1 0.1 broadcast_in_dim.26.courant
  120.2 0.0 copy-done.9
  120.2 6.0 %shard_map.73.base = f32[64,4,8,256]{3,2,1,0:T(8,128)S(1)} custom-call(f32[64,4,8,256]{3,2,1,0:T(8,128)S(1)} %bitcast.27, bf16[68,4,8,256]{3,2,1,0:T(8,128)(2,1)S(1)} %copy-done.2, bf16[68,4,8,128]{3,2,1,0:T(8,128)(2,1)S(1)} %pad_maximum_fusion.1.rim, s32[8,384]{1,0:T(8,128)S(1)} %broadcast_in_dim.23.off0, s32[8,384]{1,0:T(8,128)S(1)} %broadcast_in_dim.25.off1, ...), custom_call_target="tpu_custom_call" | custom-call | bytes 20000000 | tf_op jit(solution)/shard_map/pallas_call | solution.py:196
  126.3 0.0 copy-start.10
  126.3 1.3 copy-done.10
  127.6 11.5 %all-to-all-done.1.got = bf16[32,64,256]{2,1,0:T(8,128)(2,1)} async-done(((bf16[32,64,256]{2,1,0:T(8,128)(2,1)}), bf16[32,64,256]{2,1,0:T(8,128)(2,1)}, u32[]{:S(2)}, u32[]{:S(2)}) %all-to-all-start.1) | async-done | bytes 1048608 | tf_op jit(solution)/shard_map/all_to_all | solution.py:216
  139.1 4.6 %shard_map.80 = f32[64,4,8,256]{3,2,1,0:T(8,128)} custom-call(s32[1]{0:T(128)} %bitcast.turned, f32[64,4,8,256]{3,2,1,0:T(8,128)} %copy-done.10, f32[64,4,8,256]{3,2,1,0:T(8,128)} %bitcast.29, bf16[32,64,256]{2,1,0:T(8,128)(2,1)} %all-to-all-done.1.got), custom_call_target="tpu_custom_call" | custom-call | tf_op jit(solution)/shard_map/pallas_call | solution.py:221
  (22 shorter events, 0.0 us)
Async XLA Ops:
  6.5 0.9 copy-start
  7.4 3.2 %copy-start.14 = (bf16[64,512]{1,0:T(8,128)(2,1)}, bf16[64,512]{1,0:T(8,128)(2,1)S(1)}, u32[]{:S(2)}) copy-start(bf16[64,512]{1,0:T(8,128)(2,1)S(1)} %constant_dynamic-slice_fusion.lat) | copy-start | bytes 196612
  7.4 1.2 copy-start.13
  10.6 11.7 %copy-start.11 = (bf16[256,2048]{1,0:T(8,128)(2,1)S(1)}, bf16[256,2048]{1,0:T(8,128)(2,1)}, u32[]{:S(2)}) copy-start(bf16[256,2048]{1,0:T(8,128)(2,1)} %refs_6_.1) | copy-start | bytes 3145732
  10.6 42.2 %all-to-all-start = ((bf16[32,64,256]{2,1,0:T(8,128)(2,1)}), bf16[32,64,256]{2,1,0:T(8,128)(2,1)S(1)}, u32[]{:S(2)}, u32[]{:S(2)}) async-start(bf16[32,64,256]{2,1,0:T(8,128)(2,1)} %shard_map.74), calls=%async_computation | async-start | bytes 2097152 | tf_op jit(solution)/shard_map/all_to_all | solution.py:169
  22.3 59.8 %all-gather.2.cloned.1.call-start = ((), (), s32[]{:S(2)}) async-start(), calls=%async_computation.2 | async-start | bytes 1114112 | tf_op jit(solution)/shard_map/all_gather | solution.py:184
  22.4 25.9 %collective-permute-start.5 = (bf16[256,2048]{1,0:T(8,128)(2,1)S(1)}, bf16[256,2048]{1,0:T(8,128)(2,1)S(1)}, u32[]{:S(2)}, u32[]{:S(2)}) collective-permute-start(bf16[256,2048]{1,0:T(8,128)(2,1)S(1)} %copy-done.11), channel_id=1, source_target_pairs={{0,6},{2,4},{4,2},{6,0},{1,7},{3,5},{5,3},{7,1},{8,14},{10,12},{12... | collective-permute-start | bytes 3145736 | tf_op jit(solution)/shard_map/ppermute | solution.py:151
  27.4 5.4 %collective-permute-start = (bf16[2,4,8,256]{3,2,1,0:T(8,128)(2,1)S(1)}, bf16[2,4,8,256]{3,2,1,0:T(8,128)(2,1)S(1)}, u32[]{:S(2)}, u32[]{:S(2)}) collective-permute-start(bf16[2,4,8,256]{3,2,1,0:T(8,128)(2,1)S(1)} %get-tuple-element.9), channel_id=1, source_target_pairs={{0,8},{8,16},{16,24},{24,32},{32,40},{40,48},{48,56},{56,64},{64,7... | collective-permute-start | bytes 98312 | tf_op jit(solution)/shard_map/ppermute | solution.py:167
  30.8 5.9 %collective-permute-start.1 = (bf16[2,4,8,256]{3,2,1,0:T(8,128)(2,1)S(1)}, bf16[2,4,8,256]{3,2,1,0:T(8,128)(2,1)S(1)}, u32[]{:S(2)}, u32[]{:S(2)}) collective-permute-start(bf16[2,4,8,256]{3,2,1,0:T(8,128)(2,1)S(1)} %get-tuple-element.10), channel_id=1, source_target_pairs={{8,0},{16,8},{24,16},{32,24},{40,32},{48,40},{56,48},{64,56},{72,6... | collective-permute-start | bytes 98312 | tf_op jit(solution)/shard_map/ppermute | solution.py:168
  48.3 4.5 %copy-start.5 = (bf16[256,2048]{1,0:T(8,128)(2,1)}, bf16[256,2048]{1,0:T(8,128)(2,1)S(1)}, u32[]{:S(2)}) copy-start(bf16[256,2048]{1,0:T(8,128)(2,1)S(1)} %collective-permute-done.5.refs_1_.refs_4_.refs_7_) | copy-start | bytes 3145732
  52.8 1.0 copy-start.3
  53.8 4.1 %collective-permute-start.7 = (bf16[16,2,64,256]{3,2,1,0:T(8,128)(2,1)}, bf16[16,2,64,256]{3,2,1,0:T(8,128)(2,1)}, u32[]{:S(2)}, u32[]{:S(2)}) collective-permute-start(bf16[16,2,64,256]{3,2,1,0:T(8,128)(2,1)} %shard_map.75.refs_1_), channel_id=1, source_target_pairs={{0,1},{1,0},{2,3},{3,2},{4,5},{5,4},{6,7},{7,6},{8,9},{9,8},{10,11... | collective-permute-start | bytes 3145736 | tf_op jit(solution)/shard_map/ppermute | solution.py:173
  53.8 27.3 %collective-permute-start.6 = (bf16[16,2,64,256]{3,2,1,0:T(8,128)(2,1)}, bf16[16,2,64,256]{3,2,1,0:T(8,128)(2,1)S(1)}, u32[]{:S(2)}, u32[]{:S(2)}) collective-permute-start(bf16[16,2,64,256]{3,2,1,0:T(8,128)(2,1)} %shard_map.75.refs_1_), channel_id=1, source_target_pairs={{0,4},{4,0},{1,5},{5,1},{2,6},{6,2},{3,7},{7,3},{8,12},{12,8},{9,1... | collective-permute-start | bytes 3145736 | tf_op jit(solution)/shard_map/ppermute | solution.py:172
  56.6 37.2 %collective-permute-start.2 = (bf16[68,4,8,256]{3,2,1,0:T(8,128)(2,1)}, bf16[68,4,8,256]{3,2,1,0:T(8,128)(2,1)S(1)}, u32[]{:S(2)}, u32[]{:S(2)}) collective-permute-start(bf16[68,4,8,256]{3,2,1,0:T(8,128)(2,1)} %pad_maximum_fusion.refs_2_), channel_id=1, source_target_pairs={{0,128},{1,129},{2,130},{3,131},{4,132},{5,133},{6,134},{7,135},{8... | collective-permute-start | bytes 3342344 | tf_op jit(solution)/shard_map/ppermute | solution.py:188
  57.9 1.2 copy-start.4
  59.2 1.2 copy-start.6
  81.1 1.0 copy-start.7
  82.1 1.2 copy-start.8
  82.1 11.7 %collective-permute-start.8 = (bf16[1024,512]{1,0:T(8,128)(2,1)}, bf16[1024,512]{1,0:T(8,128)(2,1)S(1)}, u32[]{:S(2)}, u32[]{:S(2)}) collective-permute-start(bf16[1024,512]{1,0:T(8,128)(2,1)} %shard_map.78.refs_1_), channel_id=1, source_target_pairs={{0,1},{1,0},{2,3},{3,2},{4,5},{5,4},{6,7},{7,6},{8,9},{9,8},{10,11... | collective-permute-start | bytes 3145736 | tf_op jit(solution)/shard_map/ppermute | solution.py:185
  83.3 10.4 %collective-permute-start.9 = (bf16[16,2,64,256]{3,2,1,0:T(8,128)(2,1)S(1)}, bf16[16,2,64,256]{3,2,1,0:T(8,128)(2,1)S(1)}, u32[]{:S(2)}, u32[]{:S(2)}) collective-permute-start(bf16[16,2,64,256]{3,2,1,0:T(8,128)(2,1)S(1)} %copy-done.8), channel_id=1, source_target_pairs={{0,1},{1,0},{2,3},{3,2},{4,5},{5,4},{6,7},{7,6},{8,9},{9,8},{10,11... | collective-permute-start | bytes 3145736 | tf_op jit(solution)/shard_map/ppermute | solution.py:182
  93.8 1.0 copy-start.1
  94.8 1.2 copy-start.12
  101.8 7.5 %copy-start.2 = (bf16[68,4,8,256]{3,2,1,0:T(8,128)(2,1)S(1)}, bf16[68,4,8,256]{3,2,1,0:T(8,128)(2,1)}, u32[]{:S(2)}) copy-start(bf16[68,4,8,256]{3,2,1,0:T(8,128)(2,1)} %copy-done.1) | copy-start | bytes 3342340
  101.8 37.3 %all-to-all-start.1 = ((bf16[32,64,256]{2,1,0:T(8,128)(2,1)}), bf16[32,64,256]{2,1,0:T(8,128)(2,1)}, u32[]{:S(2)}, u32[]{:S(2)}) async-start(bf16[32,64,256]{2,1,0:T(8,128)(2,1)} %shard_map.79), calls=%async_computation.1 | async-start | bytes 2097152 | tf_op jit(solution)/shard_map/all_to_all | solution.py:216
  109.5 2.8 %copy-start.15 = (s32[2,8]{1,0:T(2,128)S(1)}, s32[2,8]{1,0:T(2,128)}, u32[]{:S(2)}) copy-start(s32[2,8]{1,0:T(2,128)} %param.12) | copy-start | bytes 196
  110.2 2.8 %collective-permute-start.3 = (bf16[68,4,8,2]{0,2,3,1:T(8,128)(2,1)S(1)}, bf16[68,4,8,2]{0,2,3,1:T(8,128)(2,1)S(1)}, u32[]{:S(2)}, u32[]{:S(2)}) collective-permute-start(bf16[68,4,8,2]{0,2,3,1:T(8,128)(2,1)S(1)} %copy.14), channel_id=1, source_target_pairs={{1,0},{2,1},{3,2},{4,3},{5,4},{6,5},{7,6},{0,7},{9,8},{10,9},{11,1... | collective-permute-start | bytes 26120 | tf_op jit(solution)/shard_map/ppermute | solution.py:192
  112.3 4.4 %collective-permute-start.4 = (bf16[68,4,8,2]{0,2,3,1:T(8,128)(2,1)S(1)}, bf16[68,4,8,2]{0,2,3,1:T(8,128)(2,1)S(1)}, u32[]{:S(2)}, u32[]{:S(2)}) collective-permute-start(bf16[68,4,8,2]{0,2,3,1:T(8,128)(2,1)S(1)} %copy.15), channel_id=1, source_target_pairs={{0,1},{1,2},{2,3},{3,4},{4,5},{5,6},{6,7},{7,0},{8,9},{9,10},{10,1... | collective-permute-start | bytes 26120 | tf_op jit(solution)/shard_map/ppermute | solution.py:191
  114.8 5.3 %copy-start.16 = (f32[4]{0:T(128)S(1)}, f32[4]{0:T(128)}, u32[]{:S(2)}) copy-start(f32[4]{0:T(128)} %param.13) | copy-start | bytes 52
  114.8 5.4 %copy-start.9 = (f32[64,1,4,8,256]{4,3,2,1,0:T(8,128)S(1)}, f32[64,1,4,8,256]{4,3,2,1,0:T(8,128)}, u32[]{:S(2)}) copy-start(f32[64,1,4,8,256]{4,3,2,1,0:T(8,128)} %param.9) | copy-start | bytes 6291460
  126.3 1.4 copy-start.10
Sparse Core Ops, SparseCore 0:
  25.6 56.2 all-gather.1
